TPU v7x, 512 devices: a whole 4x4x16 slice. The times are simulated.
512 devices in a mesh: dp: 32 (over z_lo, x), fsdp: 16 (over z_hi, y, core).
Axes of the slice: x: 4, y: 4, z: 16 (z_hi: 2, z_lo: 8; z = z_hi * 8 + z_lo), core: 2. Of those that a mesh axis runs over, the one named last changes fastest.
Arguments:
- hidden_in: bfloat16 [65536, 8192], P(('dp', 'fsdp')), may hold values from -6 to 6
- norm_gain: bfloat16 [8192], P('fsdp'), may hold values from 0.099609375 to 1.8984375
- value_grad: bfloat16 [65536, 512], P(('dp', 'fsdp')), may hold values from -6 to 6
- value_weight: bfloat16 [8192, 512], P('fsdp'), may hold values from -0.25 to 0.25
- proj_input: bfloat16 [8192, 64], P('fsdp'), may hold values from -0.0014648438 to 0.0014648438
- proj_output: bfloat16 [512, 64], replicated, may hold values from -0.25 to 0.25
- query_feats: float32 [1024, 4096], P(('dp', 'fsdp')), may hold values from -0.09375 to 0.09375
- example_slot: int32 [32], replicated, may hold values from 0 to 31, each once
Outputs:
- input_grad: bfloat16 [65536, 8192], P(('dp', 'fsdp'))
- gram_matrix: float32 [4096, 4096], P('dp', 'fsdp')
- scores: float32 [32, 1024], P(None, ('dp', 'fsdp'))
Inputs may be any that keep to these rules, and one draw needn't show every extreme that they name: `example_slot`: each example number appears once.
All inputs are finite; a program needn't handle non-finite values.
Results may differ from a plain program's by a relative error of at most 0.012.
Values may be sent and summed in bfloat16 or wider, within the bound.
No kernel may reach another device: no remote copies, remote signals or barrier semaphores. Data moves between devices by JAX's collectives and lax.ppermute only.
A program may use at most 64 MiB of HBM per device.

v0:
```python
import jax
import jax.numpy as jnp
from jax import lax
from jax.sharding import PartitionSpec as P


def local(
    hidden_in,
    norm_gain,
    value_grad,
    value_weight,
    proj_input,
    proj_output,
    query_feats,
    example_slot,
):
    feature_width = hidden_in.shape[1]
    wide_x = hidden_in.astype(jnp.float32)
    inverse_rms = lax.rsqrt(jnp.mean(wide_x * wide_x, axis=-1, keepdims=True) + 1e-05)
    weight_rows = lax.all_gather(value_weight, "fsdp", axis=0, tiled=True)
    factor_rows = lax.all_gather(proj_input, "fsdp", axis=0, tiled=True)
    gain_rows = lax.all_gather(norm_gain, "fsdp", axis=0, tiled=True)
    x_cols = hidden_in.astype(jnp.float32)
    normed_cols = (x_cols * inverse_rms * gain_rows.astype(jnp.float32)).astype(jnp.bfloat16)
    left_acc = jnp.dot(normed_cols, factor_rows, preferred_element_type=jnp.float32)
    block = lax.dot_general(
        value_grad, weight_rows, (((1,), (1,)), ((), ())), preferred_element_type=jnp.float32
    ).astype(jnp.bfloat16)
    left_proj = left_acc.astype(jnp.bfloat16)
    gain_wide = gain_rows.astype(jnp.float32)
    scaled = block.astype(jnp.float32) * gain_wide
    inner_sum = jnp.sum(scaled * wide_x, axis=-1, keepdims=True)
    input_grad = (
        scaled * inverse_rms - wide_x * inner_sum * inverse_rms**3 / feature_width
    ).astype(jnp.bfloat16)
    right_proj = jnp.dot(value_grad, proj_output, preferred_element_type=jnp.float32).astype(
        jnp.bfloat16
    )
    partial_grad = lax.dot_general(
        left_proj, right_proj, (((0,), (0,)), ((), ())), preferred_element_type=jnp.float32
    )
    example_feats = lax.psum(partial_grad, "fsdp").reshape(1, -1)
    feat_table = lax.all_gather(example_feats, "dp", axis=0, tiled=True)
    feat_count = feat_table.shape[1]
    row_part = feat_count // lax.axis_size("dp")
    col_part = feat_count // lax.axis_size("fsdp")
    col_start = lax.axis_index("fsdp") * col_part
    row_values = lax.dynamic_slice_in_dim(feat_table, lax.axis_index("dp") * row_part, row_part, 1)
    col_values = lax.dynamic_slice_in_dim(feat_table, col_start, col_part, 1)
    outer_terms = (row_values[:, :, None] * col_values[:, None, :]).astype(jnp.bfloat16)
    outer_terms = lax.optimization_barrier(outer_terms)
    gram_block = jnp.sum(outer_terms.astype(jnp.float32), axis=0)
    raw_scores = jnp.dot(feat_table, query_feats.T, precision=lax.Precision.HIGHEST)
    example_count = feat_table.shape[0]
    placing = (jnp.arange(example_count, dtype=jnp.int32)[:, None] == example_slot[None, :]).astype(
        jnp.float32
    )
    scores = jnp.dot(placing, raw_scores, precision=lax.Precision.HIGHEST)
    return (input_grad, gram_block, scores)


def solution(mesh):
    return jax.shard_map(
        local,
        mesh=mesh,
        in_specs=(
            P(("dp", "fsdp"), None),
            P("fsdp"),
            P(("dp", "fsdp"), None),
            P("fsdp", None),
            P("fsdp", None),
            P(),
            P(("dp", "fsdp"), None),
            P(),
        ),
        out_specs=(P(("dp", "fsdp"), None), P("dp", "fsdp"), P(None, ("dp", "fsdp"))),
        check_vma=False,
    )
```

profile of v0, /device:TPU:0, one launch (start us, length us, event | category | flops | bytes accessed | tf_op | source)
XLA Modules:
  0.0 524.5 jit_solution(14438698113956209836)
XLA Ops:
  7.2 0.0 copy-start
  7.2 0.0 all-gather.5.cloned.1.call-start
  7.2 0.7 all-gather.5.cloned.1.call-update
  7.9 0.0 all-gather.7.cloned.1.call-start
  8.0 0.7 all-gather.7.cloned.1.call-update
  8.7 0.7 reshape.29
  9.4 56.5 %all-gather = bf16[16,1,512]{2,1,0:T(2,128)(2,1)S(1)} all-gather(bf16[1,1,512]{2,1,0:T(2,128)(2,1)S(1)} %reshape.29), channel_id=1, replica_groups=mesh['dp'=32,'fsdp'=16] {'fsdp'}, dimensions={0}, use_global_device_ids=true | all-gather | bytes 17408 | tf_op jit(solution)/shard_map/all_gather | solution.py:22
  65.9 124.7 %all-gather.5.cloned.1.call-done = bf16[8192,512]{1,0:T(8,128)(2,1)} async-done(((bf16[512,512]{1,0:T(8,128)(2,1)}), bf16[8192,512]{1,0:T(8,128)(2,1)}) %all-gather.5.cloned.1.call-update) | async-done | bytes 8388624 | tf_op jit(solution)/shard_map/all_gather | solution.py:20
  190.6 0.0 copy-done
  190.6 0.0 copy-start.2
  190.6 9.0 %fusion.3 = (f32[128]{0:T(128)S(1)}, f32[128]{0:T(128)S(1)}, f32[128,8192]{1,0:T(8,128)}) fusion(bf16[128,8192]{1,0:T(8,128)(2,1)} %param.8, f32[8192]{0:T(1024)S(1)} %bitcast.17, bf16[128,512]{1,0:T(8,128)(2,1)S(1)} %copy-done, bf16[8192,512]{1,0:T(8,128)(2,1)} %all-gather.5.cloned.1.call-done), kind=kOutput, calls=%fused_computation.8 | convolution fusion | flops 1082130176 | bytes 14844928 | tf_op jit(solution)/shard_map/dot_general | solution.py:26
  199.6 0.0 copy-start.3
  199.6 61.6 %all-gather.7.cloned.1.call-done = bf16[8192,64]{0,1:T(8,128)(2,1)} async-done(((bf16[512,64]{0,1:T(8,128)(2,1)}), bf16[8192,64]{0,1:T(8,128)(2,1)}) %all-gather.7.cloned.1.call-update) | async-done | bytes 1048592 | tf_op jit(solution)/shard_map/all_gather | solution.py:21
  261.1 0.0 copy-done.2
  261.1 0.0 copy-start.4
  261.1 0.0 copy-start.5
  261.1 2.1 fusion.14
  263.3 0.0 copy-done.3
  263.3 0.3 fusion.17
  263.6 0.1 reshape.28
  263.7 122.7 %psum.7 = f32[1,4096]{1,0:T(1,128)S(1)} all-reduce(f32[1,4096]{1,0:T(1,128)S(1)} %reshape.28), channel_id=1, replica_groups=mesh['dp'=32,'fsdp'=16] {'fsdp'}, use_global_device_ids=true, to_apply=%region_2.0 | all-reduce | flops 4096 | bytes 32768 | tf_op jit(solution)/shard_map/psum | solution.py:42
  386.4 0.0 copy-start.1
  386.4 125.5 %all-gather.1 = f32[32,1,4096]{2,1,0:T(1,128)S(1)} all-gather(f32[1,1,4096]{2,1,0:T(1,128)S(1)} %bitcast.21), channel_id=1, replica_groups=mesh['dp'=32,'fsdp'=16] {'dp'}, dimensions={0}, use_global_device_ids=true | all-gather | bytes 540672 | tf_op jit(solution)/shard_map/all_gather | solution.py:43
  512.0 0.7 multiply_convert_fusion
  512.7 0.9 convert_reduce_fusion
  513.7 0.0 copy-done.4
  513.7 0.8 fusion.18
  514.4 0.0 copy-done.5
  514.4 0.7 fusion.21
  515.2 0.0 copy-done.1
  515.2 2.5 fusion.7
  (5 shorter events, 0.1 us)
Async XLA Ops:
  7.2 183.4 %copy-start = (bf16[128,512]{1,0:T(8,128)(2,1)S(1)}, bf16[128,512]{1,0:T(8,128)(2,1)}, u32[]{:S(2)}) copy-start(bf16[128,512]{1,0:T(8,128)(2,1)} %param.10) | copy-start | bytes 393220
  7.2 183.4 %all-gather.5.cloned.1.call-start = ((), (), s32[]{:S(2)}) async-start(), calls=%async_computation | async-start | bytes 8912896 | tf_op jit(solution)/shard_map/all_gather | solution.py:20
  7.9 253.2 %all-gather.7.cloned.1.call-start = ((), (), s32[]{:S(2)}) async-start(), calls=%async_computation.1 | async-start | bytes 1114112 | tf_op jit(solution)/shard_map/all_gather | solution.py:21
  190.6 70.5 %copy-start.2 = (bf16[128,8192]{1,0:T(8,128)(2,1)S(1)}, bf16[128,8192]{1,0:T(8,128)(2,1)}, u32[]{:S(2)}) copy-start(bf16[128,8192]{1,0:T(8,128)(2,1)} %param.8) | copy-start | bytes 6291460
  199.6 63.7 %copy-start.3 = (bf16[512,64]{0,1:T(8,128)(2,1)S(1)}, bf16[512,64]{0,1:T(8,128)(2,1)}, u32[]{:S(2)}) copy-start(bf16[512,64]{0,1:T(8,128)(2,1)} %param.13) | copy-start | bytes 196612
  261.1 252.5 %copy-start.4 = (f32[2,4096]{1,0:T(2,128)S(1)}, f32[2,4096]{1,0:T(2,128)}, u32[]{:S(2)}) copy-start(f32[2,4096]{1,0:T(2,128)} %param.14) | copy-start | bytes 98308
  261.1 253.3 %copy-start.5 = (s32[32]{0:T(128)S(1)}, s32[32]{0:T(128)}, u32[]{:S(2)}) copy-start(s32[32]{0:T(128)} %param.15) | copy-start | bytes 388
  386.4 128.8 %copy-start.1 = (f32[128,8192]{1,0:T(8,128)S(1)}, f32[128,8192]{1,0:T(8,128)}, u32[]{:S(2)}) copy-start(f32[128,8192]{1,0:T(8,128)} %get-tuple-element.7) | copy-start | bytes 12582916
Sparse Core Ops, SparseCore 0:
  11.3 179.2 all-gather.4
  193.7 67.3 all-gather.6
where the time goes:
time: 525 us; the launch traced here: 524 us
  blocking collectives  305 us (58%)
  waiting for transfers between devices  188 us (36%)
  between operations  14.1 us (3%)
  matrix products  12.9 us (2%)
    all_gather x1, blocking collectives, local(): feat_table = lax.all_gather(example_feats, 'dp', axis=0, tiled=True)  126 us
    all_gather x1, waiting for transfers between devices, local(): weight_rows = lax.all_gather(value_weight, 'fsdp', axis=0, tiled=True)  125 us
    psum x1, blocking collectives, local(): example_feats = lax.psum(partial_grad, 'fsdp').reshape(1, -1)  123 us
    all_gather x1, waiting for transfers between devices, local(): factor_rows = lax.all_gather(proj_input, 'fsdp', axis=0, tiled=True)  61.6 us
    all_gather x1, blocking collectives, local(): gain_rows = lax.all_gather(norm_gain, 'fsdp', axis=0, tiled=True)  56.5 us
  transfers between devices with their start and end apart: 2, of which 2 were waited for; matrix products, arithmetic and copies ran while one was open for 2% of the time, Pallas kernels for 0%

commit v1 on v0

v1 whole, which is shorter than its diff:
```python
import jax
import jax.numpy as jnp
from jax import lax
from jax.experimental import pallas as pl
from jax.experimental.pallas import tpu as pltpu
from jax.sharding import Mesh, PartitionSpec as P

F32 = jnp.float32
BF16 = jnp.bfloat16

NAMES = ("zlo", "x", "zhi", "y", "core")
DP = ("zlo", "x")
FSDP = ("zhi", "y", "core")
NEAR = ("y", "core")

NT = (((1,), (1,)), ((), ()))
TN = (((0,), (0,)), ((), ()))
VMEM = pl.BlockSpec(memory_space=pltpu.VMEM)
SMEM = pl.BlockSpec(memory_space=pltpu.SMEM)
HBM = pl.BlockSpec(memory_space=pltpu.HBM)
PARAMS = pltpu.CompilerParams(vmem_limit_bytes=24 * 1024 * 1024)


def shape(dims, dtype):
    return jax.ShapeDtypeStruct(dims, dtype)


def cost(flops, traffic):
    return pl.CostEstimate(flops=flops, bytes_accessed=traffic, transcendentals=0)


def lane_sum(value):
    total = value[:, :128]
    for at in range(128, value.shape[1], 128):
        total = total + value[:, at : at + 128]
    return total


def fold_gain(x_ref, gain_ref, p_ref, w_ref, send_ref, weight_ref):
    proj = p_ref.shape[0]
    piece = send_ref.shape[0] - proj
    gain = gain_ref[...].astype(F32)
    send_ref[:proj] = (p_ref[...].astype(F32) * gain).astype(BF16)
    for at in range(0, w_ref.shape[0], piece):
        wide = jnp.broadcast_to(gain[:, at : at + piece], (8, piece))
        column = wide.T[:, :1]
        rows = slice(at, at + piece)
        weight_ref[rows, :] = (w_ref[rows, :].astype(F32) * column).astype(BF16)
    send_ref[proj:] = weight_ref[pl.ds(pl.multiple_of(x_ref[0] * piece, piece), piece), :]


def pair_factors(send_ref, recv_ref, out_ref, rows_ref, pair_ref, sem):
    proj = pair_ref.shape[0] // 2
    pair_ref[:proj] = send_ref[:proj]
    pair_ref[proj:] = recv_ref[:proj]
    copies = [
        pltpu.make_async_copy(pair_ref, out_ref.at[at], sem.at[at])
        for at in range(out_ref.shape[0])
    ]
    for copy in copies:
        copy.start()
    rows_ref[...] = recv_ref[proj:]
    for copy in copies:
        copy.wait()


def token_stats(x_ref, v_ref, po_ref, inv_ref, right_ref):
    rows, width = x_ref.shape
    step = 512

    def body(at, acc):
        part = x_ref[:, pl.ds(pl.multiple_of(at * step, step), step)].astype(F32)
        return acc + lane_sum(part * part)

    acc = lax.fori_loop(0, width // step, body, jnp.zeros((rows, 128), F32))
    mean = jnp.sum(acc, axis=1, keepdims=True) / width
    inv_ref[...] = jnp.broadcast_to(lax.rsqrt(mean + 1e-05), inv_ref.shape)
    right_ref[...] = lax.dot_general(
        v_ref[...], po_ref[...], NT, preferred_element_type=F32
    ).astype(BF16)


def partial_feats(zhi_ref, x_ref, g_ref, inv_ref, right_ref, out_ref, rows_ref):
    near, both, depth = g_ref.shape
    proj = both // 2
    zhi = zhi_ref[0]
    acc = jnp.zeros((x_ref.shape[0], proj), F32)
    for half in range(2):
        first = (zhi if half == 0 else 1 - zhi) * near
        for at in range(near):
            cols = pl.ds(pl.multiple_of((first + at) * depth, depth), depth)
            acc = acc + lax.dot_general(
                x_ref[:, cols], g_ref[at, half * proj : (half + 1) * proj, :], NT,
                preferred_element_type=F32,
            )
    left = (acc * inv_ref[:, :1]).astype(BF16)
    rows_ref[...] = lax.dot_general(left, right_ref[...], TN, preferred_element_type=F32)
    even = rows_ref[pl.ds(0, proj // 2, stride=2), :]
    odd = rows_ref[pl.ds(1, proj // 2, stride=2), :]
    both = jnp.concatenate([even, odd], axis=1)
    for at in range(out_ref.shape[0]):
        out_ref[at] = both


def add_partials(parts_ref, out_ref):
    own = jnp.sum(parts_ref[...], axis=0).astype(BF16)
    for at in range(out_ref.shape[0]):
        out_ref[at] = own


def finish(place_ref, tab_ref, q_ref, slot_ref, gram_ref, score_ref, wide_ref):
    count = tab_ref.shape[0]
    wide_ref[...] = tab_ref[...].astype(F32)
    row, col = place_ref[0], place_ref[1]
    rows = wide_ref[:, row, :].astype(BF16)
    for k in range(2):
        cols = wide_ref[:, 2 * col + k, :].astype(BF16)
        gram_ref[:, k * 128 : (k + 1) * 128] = lax.dot_general(
            rows, cols, TN, preferred_element_type=F32
        )
    hit = slot_ref[...] == lax.broadcasted_iota(jnp.int32, (count, count), 1)
    for k in range(q_ref.shape[0]):
        terms = jnp.sum(wide_ref[...] * q_ref[k][None], axis=1)
        raw = jnp.sum(terms, axis=1, keepdims=True)
        score_ref[k : k + 1, :] = jnp.sum(jnp.where(hit, raw, 0.0), axis=0, keepdims=True)


def half_product(first, turn, x_ref, v_ref, w_ref, s_ref, held_ref, sem, acc):
    near, depth, _ = w_ref.shape
    copies = [
        pltpu.make_async_copy(w_ref.at[at], held_ref.at[at], sem.at[at]) for at in range(near)
    ]
    for copy in copies:
        copy.start()
    for at in range(near):
        copies[at].wait()
        scaled = lax.dot_general(v_ref[...], held_ref[at], NT, preferred_element_type=F32)
        s_ref[:, at * depth : (at + 1) * depth] = scaled
        for k in range(depth // 128):
            source = k if turn is None else turn[k]
            cols = pl.ds(pl.multiple_of((first + at) * depth + source * 128, 128), 128)
            acc = acc + scaled[:, k * 128 : (k + 1) * 128] * x_ref[:, cols].astype(F32)
    return acc


def near_half(spot_ref, x_ref, v_ref, w_ref, s_ref, inner_ref, held_ref, sem):
    first = spot_ref[1] * w_ref.shape[0]
    inner_ref[...] = half_product(
        first, None, x_ref, v_ref, w_ref, s_ref, held_ref, sem, jnp.zeros(inner_ref.shape, F32)
    )


def far_half(
    spot_ref, x_ref, v_ref, w_ref, s_ref, inner_ref, inv_ref, o_ref,
    held_ref, sem, far_ref, out_ref, out_sem,
):
    near, depth, _ = w_ref.shape
    width = x_ref.shape[1]
    x_at, zhi = spot_ref[0], spot_ref[1]
    across = depth // 128
    turn = [lax.rem(x_at - hop + across, across) for hop in range(across)]
    acc = half_product(
        (1 - zhi) * near, turn, x_ref, v_ref, w_ref, far_ref, held_ref, sem, inner_ref[...]
    )
    inv = inv_ref[:, :1]
    factor = jnp.sum(acc, axis=1, keepdims=True) * inv * inv * inv / width
    copies = []
    for half, source, order in ((zhi, s_ref, range(across)), (1 - zhi, far_ref, turn)):
        for at in range(near):
            start = (half * near + at) * depth
            slot = len(copies)
            for k in range(across):
                here = slice(at * depth + k * 128, at * depth + (k + 1) * 128)
                cols = pl.ds(pl.multiple_of(start + order[k] * 128, 128), 128)
                value = source[:, here] * inv - x_ref[:, cols].astype(F32) * factor
                out_ref[slot, :, pl.ds(pl.multiple_of(order[k] * 128, 128), 128)] = value.astype(
                    BF16
                )
            cols = pl.ds(pl.multiple_of(start, depth), depth)
            copy = pltpu.make_async_copy(out_ref.at[slot], o_ref.at[:, cols], out_sem.at[slot])
            copy.start()
            copies.append(copy)
    for copy in copies:
        copy.wait()


def local(
    hidden_in,
    norm_gain,
    value_grad,
    value_weight,
    proj_input,
    proj_output,
    query_feats,
    example_slot,
):
    tokens, width = hidden_in.shape
    depth, feats = value_weight.shape
    proj = proj_input.shape[1]
    lines = proj * proj // 128
    examples = lax.axis_size(DP)
    group = lax.axis_size(FSDP)
    near = group // 2
    across = lax.axis_size("x")
    piece = depth // across
    zhi = lax.axis_index("zhi").astype(jnp.int32).reshape(1)
    x_at = lax.axis_index("x").astype(jnp.int32).reshape(1)
    spot = jnp.concatenate([x_at, zhi])

    send, weight = pl.pallas_call(
        fold_gain,
        out_shape=(shape((proj + piece, depth), BF16), shape((depth, feats), BF16)),
        in_specs=[SMEM] + [VMEM] * 3,
        out_specs=(VMEM, VMEM),
        compiler_params=PARAMS,
    )(x_at, norm_gain.reshape(1, depth), proj_input.T, value_weight)
    weight_near = lax.all_gather(weight, NEAR, axis=0)
    recv = lax.ppermute(send, "zhi", [(0, 1), (1, 0)])
    pairs, rows_far = pl.pallas_call(
        pair_factors,
        out_shape=(shape((near, 2 * proj, depth), BF16), shape((piece, feats), BF16)),
        in_specs=[VMEM] * 2,
        out_specs=(HBM, VMEM),
        scratch_shapes=[
            pltpu.VMEM((2 * proj, depth), BF16),
            pltpu.SemaphoreType.DMA((near,)),
        ],
        compiler_params=PARAMS,
    )(send, recv)
    pairs = lax.all_to_all(pairs, NEAR, 0, 0, tiled=True)

    inv, right = pl.pallas_call(
        token_stats,
        out_shape=(shape((tokens, 128), F32), shape((tokens, proj), BF16)),
        in_specs=[VMEM] * 3,
        out_specs=(VMEM, VMEM),
        compiler_params=PARAMS,
        cost_estimate=cost(2 * tokens * width, 2 * tokens * width),
    )(hidden_in, value_grad, proj_output.T)

    rows_far, inv = lax.optimization_barrier((rows_far, inv))
    moved = [rows_far] + [
        lax.ppermute(rows_far, "x", [(i, (i + hop) % across) for i in range(across)])
        for hop in range(1, across)
    ]
    weight_far = lax.all_gather(jnp.concatenate(moved, axis=0), NEAR, axis=0)

    partial = pl.pallas_call(
        partial_feats,
        out_shape=shape((group, lines, 128), F32),
        in_specs=[SMEM] + [VMEM] * 4,
        out_specs=VMEM,
        scratch_shapes=[pltpu.VMEM((proj, proj), F32)],
        compiler_params=PARAMS,
    )(zhi, hidden_in, pairs, inv, right)
    partial, weight_near = lax.optimization_barrier((partial, weight_near))
    partials = lax.all_to_all(partial, FSDP, 0, 0, tiled=True)
    near_scaled, near_inner = pl.pallas_call(
        near_half,
        out_shape=(shape((tokens, near * depth), F32), shape((tokens, 128), F32)),
        in_specs=[SMEM, VMEM, VMEM, HBM],
        out_specs=(VMEM, VMEM),
        scratch_shapes=[
            pltpu.VMEM((near, depth, feats), BF16),
            pltpu.SemaphoreType.DMA((near,)),
        ],
        compiler_params=PARAMS,
        cost_estimate=cost(tokens * feats * width, feats * width),
    )(spot, hidden_in, value_grad, weight_near)
    partials, near_inner = lax.optimization_barrier((partials, near_inner))

    own = pl.pallas_call(
        add_partials,
        out_shape=shape((examples, lines, 128), BF16),
        in_specs=[VMEM],
        out_specs=VMEM,
        compiler_params=PARAMS,
    )(partials)
    table = lax.all_to_all(own, DP, 0, 0, tiled=True)
    input_grad = pl.pallas_call(
        far_half,
        out_shape=shape((tokens, width), BF16),
        in_specs=[SMEM, VMEM, VMEM, HBM, VMEM, VMEM, VMEM],
        out_specs=HBM,
        scratch_shapes=[
            pltpu.VMEM((near, depth, feats), BF16),
            pltpu.SemaphoreType.DMA((near,)),
            pltpu.VMEM((tokens, near * depth), F32),
            pltpu.VMEM((group, tokens, depth), BF16),
            pltpu.SemaphoreType.DMA((group,)),
        ],
        compiler_params=PARAMS,
        cost_estimate=cost(tokens * feats * width, 2 * feats * width),
    )(spot, hidden_in, value_grad, weight_far, near_scaled, near_inner, inv)

    place = jnp.stack([lax.axis_index(DP), lax.axis_index(FSDP)]).astype(jnp.int32)
    gram, score = pl.pallas_call(
        finish,
        out_shape=(
            shape((proj * proj // examples, proj * proj // group), F32),
            shape((query_feats.shape[0], examples), F32),
        ),
        in_specs=[SMEM] + [VMEM] * 3,
        out_specs=(VMEM, VMEM),
        scratch_shapes=[pltpu.VMEM((examples, lines, 128), F32)],
        compiler_params=PARAMS,
    )(place, table, query_feats.reshape(-1, lines, 128), example_slot.reshape(examples, 1))

    return (input_grad, gram, score.T)


def solution(mesh):
    fine = Mesh(mesh.devices.reshape(8, 4, 2, 4, 2), NAMES)
    return jax.shard_map(
        local,
        mesh=fine,
        in_specs=(
            P(NAMES, None),
            P(FSDP),
            P(NAMES, None),
            P(FSDP, None),
            P(FSDP, None),
            P(),
            P(NAMES, None),
            P(),
        ),
        out_specs=(P(NAMES, None), P(DP, FSDP), P(None, NAMES)),
        check_vma=False,
    )
```

time: 525 us -> 153 us (0.29)
  the two profiles are of different devices: /device:TPU:0 before, /device:TPU:2 now
where the time goes in v1:
time: 153 us; the launch traced here: 152 us
  starting transfers between devices  67.4 us (44%)
  waiting for transfers between devices  38.6 us (25%)
  Pallas kernels  16.2 us (11%)
  local copies, waits for them, and re-layouts  14.3 us (9%)
  between operations  14.2 us (9%)
    all_to_all x1, starting transfers between devices, local(): table = lax.all_to_all(own, DP, 0, 0, tiled=True)  24.6 us
    all_to_all x1, waiting for transfers between devices, local(): pairs = lax.all_to_all(pairs, NEAR, 0, 0, tiled=True)  16 us
    ppermute x1, starting transfers between devices, local(): recv = lax.ppermute(send, 'zhi', [(0, 1), (1, 0)])  15.7 us
    unnamed x29, local copies, waits for them, and re-layouts  13.6 us
    all_to_all x1, starting transfers between devices, local(): partials = lax.all_to_all(partial, FSDP, 0, 0, tiled=True)  12.4 us
    ppermute x3, starting transfers between devices, local(): lax.ppermute(rows_far, 'x', [(i, (i + hop) % across) for i in range(acros...  10.5 us
    all_to_all x1, waiting for transfers between devices, local(): partials = lax.all_to_all(partial, FSDP, 0, 0, tiled=True)  9.7 us
    all_to_all x1, waiting for transfers between devices, local(): table = lax.all_to_all(own, DP, 0, 0, tiled=True)  7.91 us
  transfers between devices with their start and end apart: 9, of which 6 were waited for; matrix products, arithmetic and copies ran while one was open for 1% of the time, Pallas kernels for 9%

profile of v1, /device:TPU:2, one launch (start us, length us, event | category | flops | bytes accessed | tf_op | source)
XLA Modules:
  0.0 151.8 jit_solution(6161312241327355393)
XLA Ops:
  7.2 0.0 all-gather.7.cloned.1.call-start
  7.2 0.7 reshape.23.gain_ref
  7.9 0.0 copy-start.9
  7.9 1.0 copy-done.9
  8.9 0.0 copy-start.11
  8.9 0.8 copy-done.11
  9.8 1.1 shard_map.103
  10.8 0.0 all-gather.7.cloned.1.call-update
  10.9 0.0 all-gather.5.cloned.1.call-start
  10.9 15.7 %collective-permute-start = (bf16[192,512]{1,0:T(8,128)(2,1)S(1)}, bf16[192,512]{1,0:T(8,128)(2,1)S(1)}, u32[]{:S(2)}, u32[]{:S(2)}) collective-permute-start(bf16[192,512]{1,0:T(8,128)(2,1)S(1)} %get-tuple-element.19.send_ref), channel_id=1, source_target_pairs={{0,8},{8,0},{1,9},{9,1},{2,10},{10,2},{3,11},{11,3},{4,12},{12,4},... | collective-permute-start | bytes 589832 | tf_op jit(solution)/shard_map/ppermute | solution.py:218
  26.6 0.0 copy-start
  26.7 1.6 %copy-done = bf16[128,8192]{1,0:T(8,128)(2,1)S(1)} copy-done((bf16[128,8192]{1,0:T(8,128)(2,1)S(1)}, bf16[128,8192]{1,0:T(8,128)(2,1)}, u32[]{:S(2)}) %copy-start) | copy-done | bytes 2097176
  28.2 0.0 copy-start.6
  28.2 0.9 copy-done.6
  29.1 0.0 copy-start.10
  29.1 0.8 copy-done.10
  30.0 0.7 shard_map.105
  30.7 0.0 copy-start.1
  30.7 1.2 collective-permute-done.recv_ref
  31.8 1.4 shard_map.104
  33.3 0.0 copy-start.8
  33.3 1.0 copy-done.8
  34.3 3.4 %collective-permute-start.1 = (bf16[128,512]{1,0:T(8,128)(2,1)S(1)}, bf16[128,512]{1,0:T(8,128)(2,1)S(1)}, u32[]{:S(2)}, u32[]{:S(2)}) collective-permute-start(bf16[128,512]{1,0:T(8,128)(2,1)S(1)} %get-tuple-element.22), channel_id=1, source_target_pairs={{0,16},{16,32},{32,48},{48,0},{1,17},{17,33},{33,49},{49,1},{2,18}... | collective-permute-start | bytes 393224 | tf_op jit(solution)/shard_map/ppermute | solution.py:243
  37.7 4.1 %collective-permute-start.2 = (bf16[128,512]{1,0:T(8,128)(2,1)S(1)}, bf16[128,512]{1,0:T(8,128)(2,1)S(1)}, u32[]{:S(2)}, u32[]{:S(2)}) collective-permute-start(bf16[128,512]{1,0:T(8,128)(2,1)S(1)} %get-tuple-element.22), channel_id=1, source_target_pairs={{0,32},{16,48},{32,0},{48,16},{1,33},{17,49},{33,1},{49,17},{2,34}... | collective-permute-start | bytes 393224 | tf_op jit(solution)/shard_map/ppermute | solution.py:243
  41.7 3.0 %collective-permute-start.3 = (bf16[128,512]{1,0:T(8,128)(2,1)S(1)}, bf16[128,512]{1,0:T(8,128)(2,1)S(1)}, u32[]{:S(2)}, u32[]{:S(2)}) collective-permute-start(bf16[128,512]{1,0:T(8,128)(2,1)S(1)} %get-tuple-element.22), channel_id=1, source_target_pairs={{0,48},{16,0},{32,16},{48,32},{1,49},{17,1},{33,17},{49,33},{2,50}... | collective-permute-start | bytes 393224 | tf_op jit(solution)/shard_map/ppermute | solution.py:243
  44.8 0.0 collective-permute-done.1
  44.8 2.3 %collective-permute-done.2 = bf16[128,512]{1,0:T(8,128)(2,1)S(1)} collective-permute-done((bf16[128,512]{1,0:T(8,128)(2,1)S(1)}, bf16[128,512]{1,0:T(8,128)(2,1)S(1)}, u32[]{:S(2)}, u32[]{:S(2)}) %collective-permute-start.2) | collective-permute-done | bytes 131104 | tf_op jit(solution)/shard_map/ppermute | solution.py:243
  47.1 1.5 collective-permute-done.3
  48.6 0.9 pad_maximum_fusion
  49.5 0.0 all-gather.5.cloned.1.call-update
  49.5 4.1 %all-to-all-start = ((bf16[8,128,512]{2,1,0:T(8,128)(2,1)}), bf16[8,128,512]{2,1,0:T(8,128)(2,1)S(1)}, u32[]{:S(2)}, u32[]{:S(2)}) async-start(bf16[8,128,512]{2,1,0:T(8,128)(2,1)} %copy-done.8), calls=%async_computation | async-start | bytes 2097152 | tf_op jit(solution)/shard_map/all_to_all | solution.py:230
  53.6 0.0 copy-start.7
  53.6 16.0 %all-to-all-done.g_ref = bf16[8,128,512]{2,1,0:T(8,128)(2,1)S(1)} async-done(((bf16[8,128,512]{2,1,0:T(8,128)(2,1)}), bf16[8,128,512]{2,1,0:T(8,128)(2,1)S(1)}, u32[]{:S(2)}, u32[]{:S(2)}) %all-to-all-start) | async-done | bytes 1048608 | tf_op jit(solution)/shard_map/all_to_all | solution.py:230
  69.5 0.0 copy-done.1
  69.6 1.7 %shard_map.106 = f32[16,32,128]{2,1,0:T(8,128)} custom-call(s32[1]{0:T(128)} %bitcast.1.zhi_ref, bf16[128,8192]{1,0:T(8,128)(2,1)S(1)} %copy-done.1, bf16[8,128,512]{2,1,0:T(8,128)(2,1)S(1)} %all-to-all-done.g_ref, f32[128,128]{1,0:T(8,128)S(1)} %get-tuple-element.24.inv_ref, bf16[128,64]{1,0:T(8,128)(2,1)S(1)} %get-tuple-element.25.right_ref), custom_call_target="tpu_custom_call" | custom-call | tf_op jit(solution)/shard_map/pallas_call | solution.py:248
  71.2 0.0 all-gather.7.cloned.1.call-done
  71.2 12.4 %all-to-all-start.1 = ((f32[16,32,128]{2,1,0:T(8,128)}), f32[16,32,128]{2,1,0:T(8,128)S(1)}, u32[]{:S(2)}, u32[]{:S(2)}) async-start(f32[16,32,128]{2,1,0:T(8,128)} %shard_map.106), calls=%async_computation.1 | async-start | bytes 524288 | tf_op jit(solution)/shard_map/all_to_all | solution.py:257
  83.6 0.1 pad_add_fusion.spot_ref
  83.7 0.0 copy-done.7
  83.7 0.0 copy-start.3
  83.7 2.3 %copy-done.3 = bf16[4096,512]{1,0:T(8,128)(2,1)S(1)} copy-done((bf16[4096,512]{1,0:T(8,128)(2,1)S(1)}, bf16[4096,512]{1,0:T(8,128)(2,1)}, u32[]{:S(2)}) %copy-start.3) | copy-done | bytes 4194328
  86.0 0.0 copy-start.12
  86.0 0.0 copy-start.13
  86.0 3.4 %shard_map.107 = (f32[128,4096]{1,0:T(8,128)S(1)}, f32[128,128]{1,0:T(8,128)S(1)}) custom-call(s32[2]{0:T(128)S(1)} %pad_add_fusion.spot_ref, bf16[128,8192]{1,0:T(8,128)(2,1)S(1)} %copy-done.1, bf16[128,512]{1,0:T(8,128)(2,1)S(1)} %copy-done.7, bf16[8,512,512]{2,1,0:T(8,128)(2,1)S(1)} %bitcast.15), custom_call_target="tpu_custom_call" | custom-call | flops 536870912 | bytes 4194304 | tf_op jit(solution)/shard_map/pallas_call | solution.py:258
  89.4 0.0 copy-start.4
  89.4 1.3 copy-done.4
  90.7 9.7 %all-to-all-done.1.parts_ref = f32[16,32,128]{2,1,0:T(8,128)S(1)} async-done(((f32[16,32,128]{2,1,0:T(8,128)}), f32[16,32,128]{2,1,0:T(8,128)S(1)}, u32[]{:S(2)}, u32[]{:S(2)}) %all-to-all-start.1) | async-done | bytes 262176 | tf_op jit(solution)/shard_map/all_to_all | solution.py:257
  100.4 0.7 shard_map.109
  101.1 24.6 %all-to-all-start.2 = ((bf16[32,32,128]{2,1,0:T(8,128)(2,1)}), bf16[32,32,128]{2,1,0:T(8,128)(2,1)S(1)}, u32[]{:S(2)}, u32[]{:S(2)}) async-start(bf16[32,32,128]{2,1,0:T(8,128)(2,1)} %shard_map.109), calls=%async_computation.2 | async-start | bytes 524288 | tf_op jit(solution)/shard_map/all_to_all | solution.py:279
  125.8 0.0 copy-done.12
  125.8 0.0 copy-done.13
  125.8 0.1 copy.11.slot_ref
  125.9 0.1 pad_add_fusion.1.place_ref
  126.0 0.0 all-gather.5.cloned.1.call-done
  126.0 0.0 copy-start.2
  126.0 2.2 %copy-done.2 = bf16[4096,512]{1,0:T(8,128)(2,1)S(1)} copy-done((bf16[4096,512]{1,0:T(8,128)(2,1)S(1)}, bf16[4096,512]{1,0:T(8,128)(2,1)}, u32[]{:S(2)}) %copy-start.2) | copy-done | bytes 4194328
  128.1 0.0 copy-start.5
  128.1 1.6 %copy-done.5 = f32[128,4096]{1,0:T(8,128)S(1)} copy-done((f32[128,4096]{1,0:T(8,128)S(1)}, f32[128,4096]{1,0:T(8,128)}, u32[]{:S(2)}) %copy-start.5) | copy-done | bytes 2097176
  129.7 5.8 %shard_map.108 = bf16[128,8192]{1,0:T(8,128)(2,1)} custom-call(s32[2]{0:T(128)S(1)} %pad_add_fusion.spot_ref, bf16[128,8192]{1,0:T(8,128)(2,1)S(1)} %copy-done.1, bf16[128,512]{1,0:T(8,128)(2,1)S(1)} %copy-done.7, bf16[8,512,512]{2,1,0:T(8,128)(2,1)S(1)} %bitcast.14, f32[128,4096]{1,0:T(8,128)S(1)} %copy-done.5, f32[128,128]{1,0:T(8,128)S(1)} %get-tuple-element.31.inner_ref, ...), custom_call_target="tpu_custom_call" | custom-call | flops 536870912 | bytes 8388608 | tf_op jit(solution)/shard_map/pallas_call | solution.py:280
  135.6 7.9 %all-to-all-done.2.tab_ref = bf16[32,32,128]{2,1,0:T(8,128)(2,1)S(1)} async-done(((bf16[32,32,128]{2,1,0:T(8,128)(2,1)}), bf16[32,32,128]{2,1,0:T(8,128)(2,1)S(1)}, u32[]{:S(2)}, u32[]{:S(2)}) %all-to-all-start.2) | async-done | bytes 262176 | tf_op jit(solution)/shard_map/all_to_all | solution.py:279
  143.5 1.5 shard_map.110
  (1 shorter events, 0.0 us)
Async XLA Ops:
  7.2 64.1 %all-gather.7.cloned.1.call-start = ((), (), s32[]{:S(2)}) async-start(), calls=%async_computation.4 | async-start | bytes 4718592 | tf_op jit(solution)/shard_map/all_gather | solution.py:217
  7.9 1.0 copy-start.9
  8.9 0.8 copy-start.11
  10.9 115.1 %all-gather.5.cloned.1.call-start = ((), (), s32[]{:S(2)}) async-start(), calls=%async_computation.3 | async-start | bytes 4718592 | tf_op jit(solution)/shard_map/all_gather | solution.py:246
  10.9 20.9 %collective-permute-start = (bf16[192,512]{1,0:T(8,128)(2,1)S(1)}, bf16[192,512]{1,0:T(8,128)(2,1)S(1)}, u32[]{:S(2)}, u32[]{:S(2)}) collective-permute-start(bf16[192,512]{1,0:T(8,128)(2,1)S(1)} %get-tuple-element.19.send_ref), channel_id=1, source_target_pairs={{0,8},{8,0},{1,9},{9,1},{2,10},{10,2},{3,11},{11,3},{4,12},{12,4},... | collective-permute-start | bytes 589832 | tf_op jit(solution)/shard_map/ppermute | solution.py:218
  26.6 1.6 %copy-start = (bf16[128,8192]{1,0:T(8,128)(2,1)S(1)}, bf16[128,8192]{1,0:T(8,128)(2,1)}, u32[]{:S(2)}) copy-start(bf16[128,8192]{1,0:T(8,128)(2,1)} %x_ref.7) | copy-start | bytes 6291460
  28.2 0.9 copy-start.6
  29.1 0.8 copy-start.10
  30.7 38.9 %copy-start.1 = (bf16[128,8192]{1,0:T(8,128)(2,1)S(1)}, bf16[128,8192]{1,0:T(8,128)(2,1)}, u32[]{:S(2)}) copy-start(bf16[128,8192]{1,0:T(8,128)(2,1)} %x_ref.7) | copy-start | bytes 6291460
  33.3 1.0 copy-start.8
  34.3 10.5 %collective-permute-start.1 = (bf16[128,512]{1,0:T(8,128)(2,1)S(1)}, bf16[128,512]{1,0:T(8,128)(2,1)S(1)}, u32[]{:S(2)}, u32[]{:S(2)}) collective-permute-start(bf16[128,512]{1,0:T(8,128)(2,1)S(1)} %get-tuple-element.22), channel_id=1, source_target_pairs={{0,16},{16,32},{32,48},{48,0},{1,17},{17,33},{33,49},{49,1},{2,18}... | collective-permute-start | bytes 393224 | tf_op jit(solution)/shard_map/ppermute | solution.py:243
  37.7 9.4 %collective-permute-start.2 = (bf16[128,512]{1,0:T(8,128)(2,1)S(1)}, bf16[128,512]{1,0:T(8,128)(2,1)S(1)}, u32[]{:S(2)}, u32[]{:S(2)}) collective-permute-start(bf16[128,512]{1,0:T(8,128)(2,1)S(1)} %get-tuple-element.22), channel_id=1, source_target_pairs={{0,32},{16,48},{32,0},{48,16},{1,33},{17,49},{33,1},{49,17},{2,34}... | collective-permute-start | bytes 393224 | tf_op jit(solution)/shard_map/ppermute | solution.py:243
  41.7 6.9 %collective-permute-start.3 = (bf16[128,512]{1,0:T(8,128)(2,1)S(1)}, bf16[128,512]{1,0:T(8,128)(2,1)S(1)}, u32[]{:S(2)}, u32[]{:S(2)}) collective-permute-start(bf16[128,512]{1,0:T(8,128)(2,1)S(1)} %get-tuple-element.22), channel_id=1, source_target_pairs={{0,48},{16,0},{32,16},{48,32},{1,49},{17,1},{33,17},{49,33},{2,50}... | collective-permute-start | bytes 393224 | tf_op jit(solution)/shard_map/ppermute | solution.py:243
  49.5 20.1 %all-to-all-start = ((bf16[8,128,512]{2,1,0:T(8,128)(2,1)}), bf16[8,128,512]{2,1,0:T(8,128)(2,1)S(1)}, u32[]{:S(2)}, u32[]{:S(2)}) async-start(bf16[8,128,512]{2,1,0:T(8,128)(2,1)} %copy-done.8), calls=%async_computation | async-start | bytes 2097152 | tf_op jit(solution)/shard_map/all_to_all | solution.py:230
  53.6 30.1 %copy-start.7 = (bf16[128,512]{1,0:T(8,128)(2,1)S(1)}, bf16[128,512]{1,0:T(8,128)(2,1)}, u32[]{:S(2)}) copy-start(bf16[128,512]{1,0:T(8,128)(2,1)} %v_ref.5) | copy-start | bytes 393220
  71.2 29.2 %all-to-all-start.1 = ((f32[16,32,128]{2,1,0:T(8,128)}), f32[16,32,128]{2,1,0:T(8,128)S(1)}, u32[]{:S(2)}, u32[]{:S(2)}) async-start(f32[16,32,128]{2,1,0:T(8,128)} %shard_map.106), calls=%async_computation.1 | async-start | bytes 524288 | tf_op jit(solution)/shard_map/all_to_all | solution.py:257
  83.7 2.3 %copy-start.3 = (bf16[4096,512]{1,0:T(8,128)(2,1)S(1)}, bf16[4096,512]{1,0:T(8,128)(2,1)}, u32[]{:S(2)}) copy-start(bf16[4096,512]{1,0:T(8,128)(2,1)} %all-gather.7.cloned.1.call-done) | copy-start | bytes 12582916
  86.0 39.8 %copy-start.12 = (f32[2,4096]{1,0:T(2,128)S(1)}, f32[2,4096]{1,0:T(2,128)}, u32[]{:S(2)}) copy-start(f32[2,4096]{1,0:T(2,128)} %param.14) | copy-start | bytes 98308
  86.0 39.8 %copy-start.13 = (s32[32]{0:T(128)S(1)}, s32[32]{0:T(128)}, u32[]{:S(2)}) copy-start(s32[32]{0:T(128)} %param.15) | copy-start | bytes 388
  89.4 1.3 copy-start.4
  101.1 42.3 %all-to-all-start.2 = ((bf16[32,32,128]{2,1,0:T(8,128)(2,1)}), bf16[32,32,128]{2,1,0:T(8,128)(2,1)S(1)}, u32[]{:S(2)}, u32[]{:S(2)}) async-start(bf16[32,32,128]{2,1,0:T(8,128)(2,1)} %shard_map.109), calls=%async_computation.2 | async-start | bytes 524288 | tf_op jit(solution)/shard_map/all_to_all | solution.py:279
  126.0 2.2 %copy-start.2 = (bf16[4096,512]{1,0:T(8,128)(2,1)S(1)}, bf16[4096,512]{1,0:T(8,128)(2,1)}, u32[]{:S(2)}) copy-start(bf16[4096,512]{1,0:T(8,128)(2,1)} %all-gather.5.cloned.1.call-done) | copy-start | bytes 12582916
  128.1 1.6 %copy-start.5 = (f32[128,4096]{1,0:T(8,128)S(1)}, f32[128,4096]{1,0:T(8,128)}, u32[]{:S(2)}) copy-start(f32[128,4096]{1,0:T(8,128)} %copy-done.4) | copy-start | bytes 6291460
Sparse Core Ops, SparseCore 0:
  11.0 44.2 all-gather.6
  57.4 46.2 all-gather.4

commit v2 on v1

v2 whole, which is shorter than its diff:
```python
import jax
import jax.numpy as jnp
from jax import lax
from jax.experimental import pallas as pl
from jax.experimental.pallas import tpu as pltpu
from jax.sharding import Mesh, PartitionSpec as P

F32 = jnp.float32
BF16 = jnp.bfloat16

NAMES = ("zlo", "x", "zhi", "y", "core")
DP = ("zlo", "x")
FSDP = ("zhi", "y", "core")
NEAR = ("y", "core")

NT = (((1,), (1,)), ((), ()))
TN = (((0,), (0,)), ((), ()))
VMEM = pl.BlockSpec(memory_space=pltpu.VMEM)
SMEM = pl.BlockSpec(memory_space=pltpu.SMEM)
HBM = pl.BlockSpec(memory_space=pltpu.HBM)
LARGE = pltpu.CompilerParams(vmem_limit_bytes=56 * 1024 * 1024)
PARAMS = pltpu.CompilerParams(vmem_limit_bytes=24 * 1024 * 1024)


def shape(dims, dtype):
    return jax.ShapeDtypeStruct(dims, dtype)


def cost(flops, traffic):
    return pl.CostEstimate(flops=flops, bytes_accessed=traffic, transcendentals=0)


def lane_sum(value):
    total = value[:, :128]
    for at in range(128, value.shape[1], 128):
        total = total + value[:, at : at + 128]
    return total


def token_stats(x_ref, v_ref, po_ref, inv_ref, right_ref):
    rows, width = x_ref.shape
    step = 512

    def body(at, acc):
        part = x_ref[:, pl.ds(pl.multiple_of(at * step, step), step)].astype(F32)
        return acc + lane_sum(part * part)

    acc = lax.fori_loop(0, width // step, body, jnp.zeros((rows, 128), F32))
    mean = jnp.sum(acc, axis=1, keepdims=True) / width
    inv_ref[...] = jnp.broadcast_to(lax.rsqrt(mean + 1e-05), inv_ref.shape)
    right_ref[...] = lax.dot_general(
        v_ref[...], po_ref[...], NT, preferred_element_type=F32
    ).astype(BF16)


def partial_feats(zhi_ref, x_ref, g_ref, inv_ref, right_ref, out_ref, rows_ref):
    near, both, depth = g_ref.shape
    proj = (both - 16) // 2
    zhi = zhi_ref[0]
    acc = jnp.zeros((x_ref.shape[0], proj), F32)
    for half in range(2):
        first = (zhi if half == 0 else 1 - zhi) * near
        for at in range(near):
            cols = pl.ds(pl.multiple_of((first + at) * depth, depth), depth)
            acc = acc + lax.dot_general(
                x_ref[:, cols], g_ref[at, half * proj : (half + 1) * proj, :], NT,
                preferred_element_type=F32,
            )
    left = (acc * inv_ref[:, :1]).astype(BF16)
    rows_ref[...] = lax.dot_general(left, right_ref[...], TN, preferred_element_type=F32)
    even = rows_ref[pl.ds(0, proj // 2, stride=2), :]
    odd = rows_ref[pl.ds(1, proj // 2, stride=2), :]
    out_ref[...] = jnp.concatenate([even, odd], axis=1)


def finish(place_ref, tab_ref, q_ref, slot_ref, gram_ref, score_ref, wide_ref):
    count = tab_ref.shape[0]
    wide_ref[...] = tab_ref[...].astype(F32)
    row, col = place_ref[0], place_ref[1]
    rows = wide_ref[:, row, :].astype(BF16)
    for k in range(2):
        cols = wide_ref[:, 2 * col + k, :].astype(BF16)
        gram_ref[:, k * 128 : (k + 1) * 128] = lax.dot_general(
            rows, cols, TN, preferred_element_type=F32
        )
    hit = slot_ref[...] == lax.broadcasted_iota(jnp.int32, (count, count), 1)
    for k in range(q_ref.shape[0]):
        terms = jnp.sum(wide_ref[...] * q_ref[k][None], axis=1)
        raw = jnp.sum(terms, axis=1, keepdims=True)
        score_ref[k : k + 1, :] = jnp.sum(jnp.where(hit, raw, 0.0), axis=0, keepdims=True)


def half_product(first, order, x_ref, v_ref, w_ref, g_ref, row, s_ref, held_ref, sem, acc):
    near, depth, _ = w_ref.shape
    copies = [
        pltpu.make_async_copy(w_ref.at[at], held_ref.at[at], sem.at[at]) for at in range(near)
    ]
    for copy in copies:
        copy.start()
    for at in range(near):
        copies[at].wait()
        product = lax.dot_general(v_ref[...], held_ref[at], NT, preferred_element_type=F32)
        for k in range(depth // 128):
            part = order[k] * 128
            part = part if isinstance(part, int) else pl.multiple_of(part, 128)
            gain = g_ref[at, row : row + 8, pl.ds(part, 128)][:1].astype(F32)
            scaled = product[:, k * 128 : (k + 1) * 128] * gain
            s_ref[at, :, pl.ds(part, 128)] = scaled.astype(s_ref.dtype)
            cols = pl.ds(pl.multiple_of((first + at) * depth + part, 128), 128)
            acc = acc + scaled * x_ref[:, cols].astype(F32)
    return acc


def near_half(spot_ref, x_ref, v_ref, g_ref, w_ref, s_ref, inner_ref, held_ref, sem):
    near, depth, _ = w_ref.shape
    inner_ref[...] = half_product(
        spot_ref[1] * near, range(depth // 128), x_ref, v_ref, w_ref, g_ref, g_ref.shape[1] - 16,
        s_ref, held_ref, sem, jnp.zeros(inner_ref.shape, F32),
    )


def input_gradient(
    spot_ref, x_ref, v_ref, g_ref, w_ref, s_ref, inner_ref, inv_ref, o_ref,
    held_ref, sem, far_ref, out_ref, out_sem,
):
    near, depth, _ = w_ref.shape
    width = x_ref.shape[1]
    across = depth // 128
    zhi = spot_ref[1]
    turn = [lax.rem(spot_ref[0] - hop + across, across) for hop in range(across)]
    acc = half_product(
        (1 - zhi) * near, turn, x_ref, v_ref, w_ref, g_ref, g_ref.shape[1] - 8,
        far_ref, held_ref, sem, inner_ref[...],
    )
    inv = inv_ref[...]
    total = jnp.broadcast_to(jnp.sum(acc, axis=1, keepdims=True), inv.shape)
    factor = total * inv * inv * inv / width
    stores = []
    for slot in range(2 * near):
        half, at = divmod(slot, near)
        source = s_ref if half == 0 else far_ref
        first = ((zhi if half == 0 else 1 - zhi) * near + at) * depth
        cols = pl.ds(pl.multiple_of(first, depth), depth)
        for k in range(across):
            here = slice(k * 128, (k + 1) * 128)
            some = pl.ds(pl.multiple_of(first + k * 128, 128), 128)
            out_ref[slot, :, here] = (
                source[at, :, here].astype(F32) * inv - x_ref[:, some].astype(F32) * factor
            ).astype(BF16)
        copy = pltpu.make_async_copy(out_ref.at[slot], o_ref.at[:, cols], out_sem.at[slot])
        copy.start()
        stores.append(copy)
    for copy in stores:
        copy.wait()


def local(
    hidden_in,
    norm_gain,
    value_grad,
    value_weight,
    proj_input,
    proj_output,
    query_feats,
    example_slot,
):
    tokens, width = hidden_in.shape
    depth, feats = value_weight.shape
    proj = proj_input.shape[1]
    lines = proj * proj // 128
    examples = lax.axis_size(DP)
    group = lax.axis_size(FSDP)
    near = group // 2
    across = lax.axis_size("x")
    piece = depth // across
    zhi = lax.axis_index("zhi").astype(jnp.int32).reshape(1)
    spot = jnp.concatenate([lax.axis_index("x").astype(jnp.int32).reshape(1), zhi])
    weight_near = lax.all_gather(value_weight, NEAR, axis=0)
    low = lax.axis_size("zlo")
    mirror = [
        (2 * at + half, 2 * (low - 1 - at) + 1 - half) for at in range(low) for half in range(2)
    ]
    gain = jnp.broadcast_to(norm_gain[None], (16, depth))
    rows = lax.dynamic_slice_in_dim(value_weight, lax.axis_index("x") * piece, piece, 0)
    send = jnp.concatenate([proj_input.T, gain, rows], axis=0)
    recv = lax.ppermute(send, ("zlo", "zhi"), mirror)

    inv, right = pl.pallas_call(
        token_stats,
        out_shape=(shape((tokens, 128), F32), shape((tokens, proj), BF16)),
        in_specs=[VMEM] * 3,
        out_specs=(VMEM, VMEM),
        compiler_params=PARAMS,
        cost_estimate=cost(2 * tokens * width, 2 * tokens * width),
    )(hidden_in, value_grad, proj_output.T)
    recv, inv, right = lax.optimization_barrier((recv, inv, right))
    rows_far = recv[proj + 16 :]

    def folded(part):
        return (part[:proj].astype(F32) * part[proj : proj + 1].astype(F32)).astype(BF16)

    pair = jnp.concatenate(
        [folded(send), folded(recv), send[proj : proj + 8], recv[proj : proj + 8]], axis=0
    )
    pairs = lax.all_to_all(
        jnp.broadcast_to(pair[None], (near,) + pair.shape), NEAR, 0, 0, tiled=True
    )
    moved = [rows_far] + [
        lax.ppermute(rows_far, "x", [(i, (i + hop) % across) for i in range(across)])
        for hop in range(1, across)
    ]
    moved, pairs = lax.optimization_barrier((moved, pairs))
    weight_far = lax.all_gather(jnp.concatenate(moved, axis=0), NEAR, axis=0)

    partial = pl.pallas_call(
        partial_feats,
        out_shape=shape((lines, 128), F32),
        in_specs=[SMEM] + [VMEM] * 4,
        out_specs=VMEM,
        scratch_shapes=[pltpu.VMEM((proj, proj), F32)],
        compiler_params=PARAMS,
    )(zhi, hidden_in, pairs, inv, right)
    partials = lax.all_to_all(
        jnp.broadcast_to(partial.astype(BF16)[None], (group, lines, 128)), FSDP, 0, 0, tiled=True
    )
    own = jnp.sum(partials.astype(F32), axis=0).astype(BF16)
    table = lax.all_to_all(
        jnp.broadcast_to(own[None], (examples, lines, 128)), DP, 0, 0, tiled=True
    )
    _, weight_near = lax.optimization_barrier((own, weight_near))
    near_scaled, near_inner = pl.pallas_call(
        near_half,
        out_shape=(shape((near, tokens, depth), BF16), shape((tokens, 128), F32)),
        in_specs=[SMEM] + [VMEM] * 3 + [HBM],
        out_specs=(VMEM, VMEM),
        scratch_shapes=[
            pltpu.VMEM((near, depth, feats), BF16),
            pltpu.SemaphoreType.DMA((near,)),
        ],
        compiler_params=LARGE,
        cost_estimate=cost(tokens * feats * width, feats * width),
    )(spot, hidden_in, value_grad, pairs, weight_near)
    weight_far, near_inner = lax.optimization_barrier((weight_far, near_inner))
    input_grad = pl.pallas_call(
        input_gradient,
        out_shape=shape((tokens, width), BF16),
        in_specs=[SMEM] + [VMEM] * 3 + [HBM] + [VMEM] * 3,
        out_specs=HBM,
        scratch_shapes=[
            pltpu.VMEM((near, depth, feats), BF16),
            pltpu.SemaphoreType.DMA((near,)),
            pltpu.VMEM((near, tokens, depth), F32),
            pltpu.VMEM((group, tokens, depth), BF16),
            pltpu.SemaphoreType.DMA((group,)),
        ],
        compiler_params=LARGE,
        cost_estimate=cost(tokens * feats * width, 2 * feats * width),
    )(spot, hidden_in, value_grad, pairs, weight_far, near_scaled, near_inner, inv)

    table, input_grad = lax.optimization_barrier((table, input_grad))
    place = jnp.stack([lax.axis_index(DP), lax.axis_index(FSDP)]).astype(jnp.int32)
    gram, score = pl.pallas_call(
        finish,
        out_shape=(
            shape((proj * proj // examples, proj * proj // group), F32),
            shape((query_feats.shape[0], examples), F32),
        ),
        in_specs=[SMEM] + [VMEM] * 3,
        out_specs=(VMEM, VMEM),
        scratch_shapes=[pltpu.VMEM((examples, lines, 128), F32)],
        compiler_params=PARAMS,
    )(place, table, query_feats.reshape(-1, lines, 128), example_slot.reshape(examples, 1))

    return (input_grad, gram, score.T)


def solution(mesh):
    fine = Mesh(mesh.devices.reshape(8, 4, 2, 4, 2), NAMES)
    return jax.shard_map(
        local,
        mesh=fine,
        in_specs=(
            P(NAMES, None),
            P(FSDP),
            P(NAMES, None),
            P(FSDP, None),
            P(FSDP, None),
            P(),
            P(NAMES, None),
            P(),
        ),
        out_specs=(P(NAMES, None), P(DP, FSDP), P(None, NAMES)),
        check_vma=False,
    )
```

time: 153 us -> 134 us (0.88)
  starting transfers between devices: 67.4 us -> 35.8 us
  blocking collectives: 0 us -> 28.4 us
  waiting for transfers between devices: 38.6 us -> 23.8 us
  local copies, waits for them, and re-layouts: 14.3 us -> 9.16 us
  other arithmetic: 1.04 us -> 4.64 us
    all_to_all x3 -> x2, waiting for transfers between devices: 33.6 us -> 4.74 us  [the longest x1 2.46 us: local(): lax.all_to_all(jnp.broadcast_to(own[None], (examples, lines, 128)), DP, 0...]
    all_to_all x0 -> x1, blocking collectives: none -> 28.4 us  [local(): lax.all_to_all(jnp.broadcast_to(partial.astype(BF16)[None], (group, lines...]
    all_to_all x3 -> x2, starting transfers between devices: 41.1 us -> 13.9 us  [the longest x1 9.27 us: local(): lax.all_to_all(jnp.broadcast_to(own[None], (examples, lines, 128)), DP, 0...]
    ppermute x1, waiting for transfers between devices: 1.16 us -> 14.2 us  [local(): recv = lax.ppermute(send, ('zlo', 'zhi'), mirror)]
    unnamed x29 -> x27, local copies, waits for them, and re-layouts: 13.6 us -> 4.67 us
    ppermute x1, starting transfers between devices: 15.7 us -> 11.4 us  [local(): recv = lax.ppermute(send, ('zlo', 'zhi'), mirror)]
    broadcast_in_dim x0 -> x4, local copies, waits for them, and re-layouts: none -> 2.56 us  [the longest x1 1.11 us: local(): jnp.broadcast_to(pair[None], (near,) + pair.shape)]
    pallas_call x6 -> x3, Pallas kernels: 14.1 us -> 15.6 us  [the longest x1 8.02 us: local(): pl.pallas_call(input_gradient, out_shape=shape((tokens, width), BF16), in...]
  transfers between devices with their start and end apart: 9 -> 8, of which waited for: 6 -> 5; matrix products, arithmetic and copies ran while one was open for 1% -> 7% of each run, Pallas kernels for 9% -> 12%
where the time goes in v2:
time: 134 us
  starting transfers between devices  35.8 us (27%)
  blocking collectives  28.4 us (21%)
  waiting for transfers between devices  23.8 us (18%)
  Pallas kernels  17.7 us (13%)
  between operations  14.3 us (11%)
  local copies, waits for them, and re-layouts  9.16 us (7%)
  other arithmetic  4.64 us (3%)
    all_to_all x1, blocking collectives, local(): lax.all_to_all(jnp.broadcast_to(partial.astype(BF16)[None], (group, lines...  28.4 us
    ppermute x1, waiting for transfers between devices, local(): recv = lax.ppermute(send, ('zlo', 'zhi'), mirror)  14.2 us
    ppermute x1, starting transfers between devices, local(): recv = lax.ppermute(send, ('zlo', 'zhi'), mirror)  11.4 us
    ppermute x3, starting transfers between devices, local(): lax.ppermute(rows_far, 'x', [(i, (i + hop) % across) for i in range(acros...  10.5 us
    all_to_all x1, starting transfers between devices, local(): lax.all_to_all(jnp.broadcast_to(own[None], (examples, lines, 128)), DP, 0...  9.27 us
    pallas_call x1, Pallas kernels, local(): pl.pallas_call(input_gradient, out_shape=shape((tokens, width), BF16), in...  8.02 us
    pallas_call x1, Pallas kernels, local(): pl.pallas_call(near_half, out_shape=(shape((near, tokens, depth), BF16),...  6.66 us
    unnamed x27, local copies, waits for them, and re-layouts  4.67 us
  transfers between devices with their start and end apart: 8, of which 5 were waited for; matrix products, arithmetic and copies ran while one was open for 7% of the time, Pallas kernels for 12%

profile of v2, /device:TPU:2, one launch (start us, length us, event | category | flops | bytes accessed | tf_op | source)
XLA Modules:
  0.0 133.8 jit_solution(8183686050364112723)
XLA Ops:
  7.2 0.0 copy-start.11
  7.2 0.0 copy-start.6
  7.2 0.0 all-gather.7.cloned.1.call-start
  7.2 0.7 all-gather.7.cloned.1.call-update
  7.9 0.9 constant_dynamic-slice_fusion
  8.8 0.7 broadcast_in_dim.8
  9.5 0.9 pad_maximum_fusion.1
  10.4 11.4 %collective-permute-start = (bf16[208,512]{1,0:T(8,128)(2,1)S(1)}, bf16[208,512]{1,0:T(8,128)(2,1)S(1)}, u32[]{:S(2)}, u32[]{:S(2)}) collective-permute-start(bf16[208,512]{1,0:T(8,128)(2,1)S(1)} %pad_maximum_fusion.1), channel_id=1, source_target_pairs={{0,456},{8,448},{64,392},{72,384},{128,328},{136,320},{192,264},{2... | collective-permute-start | bytes 638984 | tf_op jit(solution)/shard_map/ppermute | solution.py:186
  21.8 0.7 convert_element_type.25
  22.5 0.0 copy-start
  22.5 1.6 %copy-done = bf16[128,8192]{1,0:T(8,128)(2,1)S(1)} copy-done((bf16[128,8192]{1,0:T(8,128)(2,1)S(1)}, bf16[128,8192]{1,0:T(8,128)(2,1)}, u32[]{:S(2)}) %copy-start) | copy-done | bytes 2097176
  24.1 0.0 copy-start.3
  24.1 0.9 copy-done.3
  25.0 0.0 copy-start.5
  25.0 0.8 copy-done.5
  25.8 0.7 shard_map.103
  26.5 0.0 copy-done.6
  26.5 0.0 copy-start.4
  26.5 14.2 %collective-permute-done = bf16[208,512]{1,0:T(8,128)(2,1)S(1)} collective-permute-done((bf16[208,512]{1,0:T(8,128)(2,1)S(1)}, bf16[208,512]{1,0:T(8,128)(2,1)S(1)}, u32[]{:S(2)}, u32[]{:S(2)}) %collective-permute-start) | collective-permute-done | bytes 213024 | tf_op jit(solution)/shard_map/ppermute | solution.py:186
  40.7 0.0 copy-start.7
  40.8 0.0 copy-done.11
  40.8 0.6 copy-done.7
  41.4 1.1 broadcast_in_dim.9
  42.6 0.0 copy-start.1
  42.6 4.6 %all-to-all-start = ((bf16[8,144,512]{2,1,0:T(8,128)(2,1)}), bf16[8,144,512]{2,1,0:T(8,128)(2,1)S(1)}, u32[]{:S(2)}, u32[]{:S(2)}) async-start(bf16[8,144,512]{2,1,0:T(8,128)(2,1)} %broadcast_in_dim.9), calls=%async_computation | async-start | bytes 2359296 | tf_op jit(solution)/shard_map/all_to_all | solution.py:205
  47.2 0.0 all-gather.5.cloned.1.call-start
  47.2 0.9 slice.16
  48.1 3.4 %collective-permute-start.1 = (bf16[128,512]{1,0:T(8,128)(2,1)S(1)}, bf16[128,512]{1,0:T(8,128)(2,1)S(1)}, u32[]{:S(2)}, u32[]{:S(2)}) collective-permute-start(bf16[128,512]{1,0:T(8,128)(2,1)S(1)} %slice.16), channel_id=1, source_target_pairs={{0,16},{16,32},{32,48},{48,0},{1,17},{17,33},{33,49},{49,1},{2,18}... | collective-permute-start | bytes 393224 | tf_op jit(solution)/shard_map/ppermute | solution.py:209
  51.5 3.0 %collective-permute-start.2 = (bf16[128,512]{1,0:T(8,128)(2,1)S(1)}, bf16[128,512]{1,0:T(8,128)(2,1)S(1)}, u32[]{:S(2)}, u32[]{:S(2)}) collective-permute-start(bf16[128,512]{1,0:T(8,128)(2,1)S(1)} %slice.16), channel_id=1, source_target_pairs={{0,32},{16,48},{32,0},{48,16},{1,33},{17,49},{33,1},{49,17},{2,34}... | collective-permute-start | bytes 393224 | tf_op jit(solution)/shard_map/ppermute | solution.py:209
  54.6 4.1 %collective-permute-start.3 = (bf16[128,512]{1,0:T(8,128)(2,1)S(1)}, bf16[128,512]{1,0:T(8,128)(2,1)}, u32[]{:S(2)}, u32[]{:S(2)}) collective-permute-start(bf16[128,512]{1,0:T(8,128)(2,1)S(1)} %slice.16), channel_id=1, source_target_pairs={{0,48},{16,0},{32,16},{48,32},{1,49},{17,1},{33,17},{49,33},{2,50}... | collective-permute-start | bytes 393224 | tf_op jit(solution)/shard_map/ppermute | solution.py:209
  58.6 0.0 collective-permute-done.1
  58.6 0.0 copy-start.8
  58.6 2.6 %collective-permute-done.2 = bf16[128,512]{1,0:T(8,128)(2,1)S(1)} collective-permute-done((bf16[128,512]{1,0:T(8,128)(2,1)S(1)}, bf16[128,512]{1,0:T(8,128)(2,1)S(1)}, u32[]{:S(2)}, u32[]{:S(2)}) %collective-permute-start.2) | collective-permute-done | bytes 131104 | tf_op jit(solution)/shard_map/ppermute | solution.py:209
  61.3 0.0 copy-done.8
  61.3 0.0 copy-start.9
  61.3 0.7 copy-done.9
  61.9 1.5 %collective-permute-done.3 = bf16[128,512]{1,0:T(8,128)(2,1)} collective-permute-done((bf16[128,512]{1,0:T(8,128)(2,1)S(1)}, bf16[128,512]{1,0:T(8,128)(2,1)}, u32[]{:S(2)}, u32[]{:S(2)}) %collective-permute-start.3) | collective-permute-done | bytes 131104 | tf_op jit(solution)/shard_map/ppermute | solution.py:209
  63.4 2.3 %all-to-all-done.g_ref = bf16[8,144,512]{2,1,0:T(8,128)(2,1)S(1)} async-done(((bf16[8,144,512]{2,1,0:T(8,128)(2,1)}), bf16[8,144,512]{2,1,0:T(8,128)(2,1)S(1)}, u32[]{:S(2)}, u32[]{:S(2)}) %all-to-all-start) | async-done | bytes 1179680 | tf_op jit(solution)/shard_map/all_to_all | solution.py:205
  65.7 0.0 copy-start.2
  65.7 2.3 %pad_maximum_fusion = bf16[512,512]{1,0:T(8,128)(2,1)} fusion(bf16[128,512]{1,0:T(8,128)(2,1)} %collective-permute-done.3, bf16[128,512]{1,0:T(8,128)(2,1)} %copy-done.9, bf16[128,512]{1,0:T(8,128)(2,1)} %copy-done.8, bf16[128,512]{1,0:T(8,128)(2,1)S(1)} %slice.16), kind=kLoop, calls=%fused_computation | loop fusion | flops 2097152 | bytes 1048576 | tf_op jit(solution)/shard_map/concatenate | solution.py:213
  68.0 0.0 all-gather.5.cloned.1.call-update
  68.0 0.0 copy-done.4
  68.0 0.0 copy-done.1
  68.1 0.0 copy-start.10
  68.1 0.0 copy-start.12
  68.1 0.9 shard_map.104
  69.0 0.0 copy-done.2
  69.1 28.4 %all_to_all.15 = bf16[16,32,128]{2,1,0:T(8,128)(2,1)S(1)} all-to-all(bf16[16,32,128]{2,1,0:T(8,128)(2,1)S(1)} %broadcast_in_dim.10), channel_id=1, replica_groups=mesh['zlo'=8,'x'=4,'zhi'=2,'y'=4,'core'=2] {'zhi','y','core'}, dimensions={0} | all-to-all | bytes 262144 | tf_op jit(solution)/shard_map/all_to_all | solution.py:223
  97.5 0.7 broadcast_in_dim.11
  98.2 9.3 %all-to-all-start.2 = ((bf16[32,32,128]{2,1,0:T(8,128)(2,1)}), bf16[32,32,128]{2,1,0:T(8,128)(2,1)S(1)}, u32[]{:S(2)}, u32[]{:S(2)}) async-start(bf16[32,32,128]{2,1,0:T(8,128)(2,1)} %broadcast_in_dim.11), calls=%async_computation.2 | async-start | bytes 524288 | tf_op jit(solution)/shard_map/all_to_all | solution.py:227
  107.5 0.0 copy-done.10
  107.5 0.0 copy-done.12
  107.5 0.1 copy.12.slot_ref
  107.6 0.7 pad_add_fusion.spot_ref
  108.3 0.1 pad_add_fusion.1.place_ref
  108.4 0.0 all-gather.7.cloned.1.call-done
  108.4 6.7 %shard_map.105 = (bf16[8,128,512]{2,1,0:T(8,128)(2,1)}, f32[128,128]{1,0:T(8,128)}) custom-call(s32[2]{0:T(128)} %pad_add_fusion.spot_ref, bf16[128,8192]{1,0:T(8,128)(2,1)} %x_ref.7, bf16[128,512]{1,0:T(8,128)(2,1)} %v_ref.5, bf16[8,144,512]{2,1,0:T(8,128)(2,1)} %copy-done.2, bf16[8,512,512]{2,1,0:T(8,128)(2,1)} %bitcast.18), custom_call_target="tpu_custom_call" | custom-call | flops 536870912 | bytes 4194304 | tf_op jit(solution)/shard_map/pallas_call | solution.py:231
  115.0 0.0 all-gather.5.cloned.1.call-done
  115.1 8.0 %shard_map.106 = bf16[128,8192]{1,0:T(8,128)(2,1)} custom-call(s32[2]{0:T(128)} %pad_add_fusion.spot_ref, bf16[128,8192]{1,0:T(8,128)(2,1)} %x_ref.7, bf16[128,512]{1,0:T(8,128)(2,1)} %v_ref.5, bf16[8,144,512]{2,1,0:T(8,128)(2,1)} %copy-done.2, bf16[8,512,512]{2,1,0:T(8,128)(2,1)} %bitcast.19, bf16[8,128,512]{2,1,0:T(8,128)(2,1)} %get-tuple-element.35.s_ref, ...), custom_call_target="tpu_custom_call" | custom-call | flops 536870912 | bytes 8388608 | tf_op jit(solution)/shard_map/pallas_call | solution.py:244
  123.1 2.5 %all-to-all-done.2.tab_ref = bf16[32,32,128]{2,1,0:T(8,128)(2,1)S(1)} async-done(((bf16[32,32,128]{2,1,0:T(8,128)(2,1)}), bf16[32,32,128]{2,1,0:T(8,128)(2,1)S(1)}, u32[]{:S(2)}, u32[]{:S(2)}) %all-to-all-start.2) | async-done | bytes 262176 | tf_op jit(solution)/shard_map/all_to_all | solution.py:227
  125.6 1.5 %shard_map.107 = (f32[128,256]{1,0:T(8,128)}, f32[2,32]{1,0:T(2,128)}) custom-call(s32[2]{0:T(128)S(1)} %pad_add_fusion.1.place_ref, bf16[32,32,128]{2,1,0:T(8,128)(2,1)S(1)} %all-to-all-done.2.tab_ref, f32[2,32,128]{2,1,0:T(8,128)S(1)} %bitcast.16, s32[32,1]{1,0:T(8,128)S(1)} %copy.12.slot_ref), custom_call_target="tpu_custom_call" | custom-call | tf_op jit(solution)/shard_map/pallas_call | solution.py:262
  (10 shorter events, 0.1 us)
Async XLA Ops:
  7.2 33.6 %copy-start.11 = (bf16[512]{0:T(512)(128)(2,1)S(1)}, bf16[512]{0:T(512)(128)(2,1)}, u32[]{:S(2)}) copy-start(bf16[512]{0:T(512)(128)(2,1)} %param.9) | copy-start | bytes 3076
  7.2 19.3 %copy-start.6 = (bf16[512,64]{0,1:T(8,128)(2,1)S(1)}, bf16[512,64]{0,1:T(8,128)(2,1)}, u32[]{:S(2)}) copy-start(bf16[512,64]{0,1:T(8,128)(2,1)} %param.12) | copy-start | bytes 196612
  7.2 101.2 %all-gather.7.cloned.1.call-start = ((), (), s32[]{:S(2)}) async-start(), calls=%async_computation.4 | async-start | bytes 4718592 | tf_op jit(solution)/shard_map/all_gather | solution.py:178
  10.4 30.3 %collective-permute-start = (bf16[208,512]{1,0:T(8,128)(2,1)S(1)}, bf16[208,512]{1,0:T(8,128)(2,1)S(1)}, u32[]{:S(2)}, u32[]{:S(2)}) collective-permute-start(bf16[208,512]{1,0:T(8,128)(2,1)S(1)} %pad_maximum_fusion.1), channel_id=1, source_target_pairs={{0,456},{8,448},{64,392},{72,384},{128,328},{136,320},{192,264},{2... | collective-permute-start | bytes 638984 | tf_op jit(solution)/shard_map/ppermute | solution.py:186
  22.5 1.6 %copy-start = (bf16[128,8192]{1,0:T(8,128)(2,1)S(1)}, bf16[128,8192]{1,0:T(8,128)(2,1)}, u32[]{:S(2)}) copy-start(bf16[128,8192]{1,0:T(8,128)(2,1)} %x_ref.7) | copy-start | bytes 6291460
  24.1 0.9 copy-start.3
  25.0 0.8 copy-start.5
  26.5 41.5 %copy-start.4 = (f32[128,128]{1,0:T(8,128)}, f32[128,128]{1,0:T(8,128)S(1)}, u32[]{:S(2)}) copy-start(f32[128,128]{1,0:T(8,128)S(1)} %get-tuple-element.26.inv_ref) | copy-start | bytes 196612
  40.7 0.7 copy-start.7
  42.6 25.5 %copy-start.1 = (bf16[128,8192]{1,0:T(8,128)(2,1)S(1)}, bf16[128,8192]{1,0:T(8,128)(2,1)}, u32[]{:S(2)}) copy-start(bf16[128,8192]{1,0:T(8,128)(2,1)} %x_ref.7) | copy-start | bytes 6291460
  42.6 23.2 %all-to-all-start = ((bf16[8,144,512]{2,1,0:T(8,128)(2,1)}), bf16[8,144,512]{2,1,0:T(8,128)(2,1)S(1)}, u32[]{:S(2)}, u32[]{:S(2)}) async-start(bf16[8,144,512]{2,1,0:T(8,128)(2,1)} %broadcast_in_dim.9), calls=%async_computation | async-start | bytes 2359296 | tf_op jit(solution)/shard_map/all_to_all | solution.py:205
  47.2 67.9 %all-gather.5.cloned.1.call-start = ((), (), s32[]{:S(2)}) async-start(), calls=%async_computation.3 | async-start | bytes 4718592 | tf_op jit(solution)/shard_map/all_gather | solution.py:213
  48.1 10.5 %collective-permute-start.1 = (bf16[128,512]{1,0:T(8,128)(2,1)S(1)}, bf16[128,512]{1,0:T(8,128)(2,1)S(1)}, u32[]{:S(2)}, u32[]{:S(2)}) collective-permute-start(bf16[128,512]{1,0:T(8,128)(2,1)S(1)} %slice.16), channel_id=1, source_target_pairs={{0,16},{16,32},{32,48},{48,0},{1,17},{17,33},{33,49},{49,1},{2,18}... | collective-permute-start | bytes 393224 | tf_op jit(solution)/shard_map/ppermute | solution.py:209
  51.5 9.7 %collective-permute-start.2 = (bf16[128,512]{1,0:T(8,128)(2,1)S(1)}, bf16[128,512]{1,0:T(8,128)(2,1)S(1)}, u32[]{:S(2)}, u32[]{:S(2)}) collective-permute-start(bf16[128,512]{1,0:T(8,128)(2,1)S(1)} %slice.16), channel_id=1, source_target_pairs={{0,32},{16,48},{32,0},{48,16},{1,33},{17,49},{33,1},{49,17},{2,34}... | collective-permute-start | bytes 393224 | tf_op jit(solution)/shard_map/ppermute | solution.py:209
  54.6 8.9 %collective-permute-start.3 = (bf16[128,512]{1,0:T(8,128)(2,1)S(1)}, bf16[128,512]{1,0:T(8,128)(2,1)}, u32[]{:S(2)}, u32[]{:S(2)}) collective-permute-start(bf16[128,512]{1,0:T(8,128)(2,1)S(1)} %slice.16), channel_id=1, source_target_pairs={{0,48},{16,0},{32,16},{48,32},{1,49},{17,1},{33,17},{49,33},{2,50}... | collective-permute-start | bytes 393224 | tf_op jit(solution)/shard_map/ppermute | solution.py:209
  58.6 2.6 %copy-start.8 = (bf16[128,512]{1,0:T(8,128)(2,1)}, bf16[128,512]{1,0:T(8,128)(2,1)S(1)}, u32[]{:S(2)}) copy-start(bf16[128,512]{1,0:T(8,128)(2,1)S(1)} %collective-permute-done.1) | copy-start | bytes 393220
  61.3 0.7 copy-start.9
  65.7 3.3 %copy-start.2 = (bf16[8,144,512]{2,1,0:T(8,128)(2,1)}, bf16[8,144,512]{2,1,0:T(8,128)(2,1)S(1)}, u32[]{:S(2)}) copy-start(bf16[8,144,512]{2,1,0:T(8,128)(2,1)S(1)} %all-to-all-done.g_ref) | copy-start | bytes 3538948
  68.1 39.5 %copy-start.10 = (f32[2,4096]{1,0:T(2,128)S(1)}, f32[2,4096]{1,0:T(2,128)}, u32[]{:S(2)}) copy-start(f32[2,4096]{1,0:T(2,128)} %param.14) | copy-start | bytes 98308
  68.1 39.5 %copy-start.12 = (s32[32]{0:T(128)S(1)}, s32[32]{0:T(128)}, u32[]{:S(2)}) copy-start(s32[32]{0:T(128)} %param.15) | copy-start | bytes 388
  98.2 27.3 %all-to-all-start.2 = ((bf16[32,32,128]{2,1,0:T(8,128)(2,1)}), bf16[32,32,128]{2,1,0:T(8,128)(2,1)S(1)}, u32[]{:S(2)}, u32[]{:S(2)}) async-start(bf16[32,32,128]{2,1,0:T(8,128)(2,1)} %broadcast_in_dim.11), calls=%async_computation.2 | async-start | bytes 524288 | tf_op jit(solution)/shard_map/all_to_all | solution.py:227
Sparse Core Ops, SparseCore 0:
  10.2 46.7 all-gather.6
  68.1 40.3 all-gather.4

commit v3 on v2

--- a/solution.py
+++ b/solution.py
@@ -209,8 +209,9 @@
         lax.ppermute(rows_far, "x", [(i, (i + hop) % across) for i in range(across)])
         for hop in range(1, across)
     ]
-    moved, pairs = lax.optimization_barrier((moved, pairs))
-    weight_far = lax.all_gather(jnp.concatenate(moved, axis=0), NEAR, axis=0)
+    shard_far = jnp.concatenate(moved, axis=0)
+    shard_far, pairs = lax.optimization_barrier((shard_far, pairs))
+    weight_far = lax.all_gather(shard_far, NEAR, axis=0)
 
     partial = pl.pallas_call(
         partial_feats,

time: 134 us -> 132 us (0.985)
  other arithmetic: 4.64 us -> 3.14 us
    concatenate x1, other arithmetic: 2.28 us -> 0.83 us  [local(): shard_far = jnp.concatenate(moved, axis=0)]
    unnamed x27 -> x23, local copies, waits for them, and re-layouts: 4.67 us -> 4 us
  transfers between devices with their start and end apart: 8 -> 8, of which waited for: 5 -> 5; matrix products, arithmetic and copies ran while one was open for 7% -> 6% of each run, Pallas kernels for 12% -> 12%
where the time goes in v3:
time: 132 us
  starting transfers between devices  35.8 us (27%)
  blocking collectives  28.4 us (22%)
  waiting for transfers between devices  23.7 us (18%)
  Pallas kernels  17.8 us (13%)
  between operations  14.3 us (11%)
  local copies, waits for them, and re-layouts  8.47 us (6%)
  other arithmetic  3.14 us (2%)
    all_to_all x1, blocking collectives, local(): lax.all_to_all(jnp.broadcast_to(partial.astype(BF16)[None], (group, lines...  28.4 us
    ppermute x1, waiting for transfers between devices, local(): recv = lax.ppermute(send, ('zlo', 'zhi'), mirror)  14.2 us
    ppermute x1, starting transfers between devices, local(): recv = lax.ppermute(send, ('zlo', 'zhi'), mirror)  11.4 us
    ppermute x3, starting transfers between devices, local(): lax.ppermute(rows_far, 'x', [(i, (i + hop) % across) for i in range(acros...  10.5 us
    all_to_all x1, starting transfers between devices, local(): lax.all_to_all(jnp.broadcast_to(own[None], (examples, lines, 128)), DP, 0...  9.27 us
    pallas_call x1, Pallas kernels, local(): pl.pallas_call(input_gradient, out_shape=shape((tokens, width), BF16), in...  8.03 us
    pallas_call x1, Pallas kernels, local(): pl.pallas_call(near_half, out_shape=(shape((near, tokens, depth), BF16),...  6.67 us
    ppermute x3, waiting for transfers between devices, local(): lax.ppermute(rows_far, 'x', [(i, (i + hop) % across) for i in range(acros...  4.69 us
  transfers between devices with their start and end apart: 8, of which 5 were waited for; matrix products, arithmetic and copies ran while one was open for 6% of the time, Pallas kernels for 12%

profile of v3, /device:TPU:2, one launch (start us, length us, event | category | flops | bytes accessed | tf_op | source)
XLA Modules:
  0.0 131.6 jit_solution(3260500237646752158)
XLA Ops:
  7.2 0.0 copy-start.9
  7.2 0.0 copy-start.6
  7.2 0.0 all-gather.7.cloned.1.call-start
  7.2 0.7 all-gather.7.cloned.1.call-update
  7.9 0.9 constant_dynamic-slice_fusion
  8.8 0.7 broadcast_in_dim.8
  9.5 0.9 pad_maximum_fusion.1
  10.4 11.4 %collective-permute-start = (bf16[208,512]{1,0:T(8,128)(2,1)S(1)}, bf16[208,512]{1,0:T(8,128)(2,1)S(1)}, u32[]{:S(2)}, u32[]{:S(2)}) collective-permute-start(bf16[208,512]{1,0:T(8,128)(2,1)S(1)} %pad_maximum_fusion.1), channel_id=1, source_target_pairs={{0,456},{8,448},{64,392},{72,384},{128,328},{136,320},{192,264},{2... | collective-permute-start | bytes 638984 | tf_op jit(solution)/shard_map/ppermute | solution.py:186
  21.8 0.7 convert_element_type.25
  22.5 0.0 copy-start
  22.5 1.6 %copy-done = bf16[128,8192]{1,0:T(8,128)(2,1)S(1)} copy-done((bf16[128,8192]{1,0:T(8,128)(2,1)S(1)}, bf16[128,8192]{1,0:T(8,128)(2,1)}, u32[]{:S(2)}) %copy-start) | copy-done | bytes 2097176
  24.1 0.0 copy-start.3
  24.1 0.9 copy-done.3
  25.0 0.0 copy-start.5
  25.0 0.8 copy-done.5
  25.8 0.7 shard_map.103
  26.5 0.0 copy-done.6
  26.5 0.0 copy-start.4
  26.5 14.2 %collective-permute-done = bf16[208,512]{1,0:T(8,128)(2,1)S(1)} collective-permute-done((bf16[208,512]{1,0:T(8,128)(2,1)S(1)}, bf16[208,512]{1,0:T(8,128)(2,1)S(1)}, u32[]{:S(2)}, u32[]{:S(2)}) %collective-permute-start) | collective-permute-done | bytes 213024 | tf_op jit(solution)/shard_map/ppermute | solution.py:186
  40.7 0.0 copy-start.7
  40.8 0.0 copy-done.9
  40.8 0.6 copy-done.7
  41.4 1.1 broadcast_in_dim.9
  42.5 0.0 copy-start.1
  42.5 4.6 %all-to-all-start = ((bf16[8,144,512]{2,1,0:T(8,128)(2,1)}), bf16[8,144,512]{2,1,0:T(8,128)(2,1)S(1)}, u32[]{:S(2)}, u32[]{:S(2)}) async-start(bf16[8,144,512]{2,1,0:T(8,128)(2,1)} %broadcast_in_dim.9), calls=%async_computation | async-start | bytes 2359296 | tf_op jit(solution)/shard_map/all_to_all | solution.py:205
  47.1 0.0 all-gather.5.cloned.1.call-start
  47.2 0.9 slice.16
  48.1 3.4 %collective-permute-start.1 = (bf16[128,512]{1,0:T(8,128)(2,1)S(1)}, bf16[128,512]{1,0:T(8,128)(2,1)S(1)}, u32[]{:S(2)}, u32[]{:S(2)}) collective-permute-start(bf16[128,512]{1,0:T(8,128)(2,1)S(1)} %slice.16), channel_id=1, source_target_pairs={{0,16},{16,32},{32,48},{48,0},{1,17},{17,33},{33,49},{49,1},{2,18}... | collective-permute-start | bytes 393224 | tf_op jit(solution)/shard_map/ppermute | solution.py:209
  51.5 3.0 %collective-permute-start.2 = (bf16[128,512]{1,0:T(8,128)(2,1)S(1)}, bf16[128,512]{1,0:T(8,128)(2,1)S(1)}, u32[]{:S(2)}, u32[]{:S(2)}) collective-permute-start(bf16[128,512]{1,0:T(8,128)(2,1)S(1)} %slice.16), channel_id=1, source_target_pairs={{0,32},{16,48},{32,0},{48,16},{1,33},{17,49},{33,1},{49,17},{2,34}... | collective-permute-start | bytes 393224 | tf_op jit(solution)/shard_map/ppermute | solution.py:209
  54.5 4.1 %collective-permute-start.3 = (bf16[128,512]{1,0:T(8,128)(2,1)S(1)}, bf16[128,512]{1,0:T(8,128)(2,1)S(1)}, u32[]{:S(2)}, u32[]{:S(2)}) collective-permute-start(bf16[128,512]{1,0:T(8,128)(2,1)S(1)} %slice.16), channel_id=1, source_target_pairs={{0,48},{16,0},{32,16},{48,32},{1,49},{17,1},{33,17},{49,33},{2,50}... | collective-permute-start | bytes 393224 | tf_op jit(solution)/shard_map/ppermute | solution.py:209
  58.6 0.0 collective-permute-done.1
  58.6 2.6 %collective-permute-done.2 = bf16[128,512]{1,0:T(8,128)(2,1)S(1)} collective-permute-done((bf16[128,512]{1,0:T(8,128)(2,1)S(1)}, bf16[128,512]{1,0:T(8,128)(2,1)S(1)}, u32[]{:S(2)}, u32[]{:S(2)}) %collective-permute-start.2) | collective-permute-done | bytes 131104 | tf_op jit(solution)/shard_map/ppermute | solution.py:209
  61.2 2.1 %collective-permute-done.3 = bf16[128,512]{1,0:T(8,128)(2,1)S(1)} collective-permute-done((bf16[128,512]{1,0:T(8,128)(2,1)S(1)}, bf16[128,512]{1,0:T(8,128)(2,1)S(1)}, u32[]{:S(2)}, u32[]{:S(2)}) %collective-permute-start.3) | collective-permute-done | bytes 131104 | tf_op jit(solution)/shard_map/ppermute | solution.py:209
  63.3 0.8 pad_maximum_fusion
  64.1 1.6 %all-to-all-done.g_ref = bf16[8,144,512]{2,1,0:T(8,128)(2,1)S(1)} async-done(((bf16[8,144,512]{2,1,0:T(8,128)(2,1)}), bf16[8,144,512]{2,1,0:T(8,128)(2,1)S(1)}, u32[]{:S(2)}, u32[]{:S(2)}) %all-to-all-start) | async-done | bytes 1179680 | tf_op jit(solution)/shard_map/all_to_all | solution.py:205
  65.7 0.0 copy-start.2
  65.7 0.0 all-gather.5.cloned.1.call-update
  65.7 0.0 copy-done.4
  65.8 0.0 copy-done.1
  65.8 0.0 copy-start.8
  65.8 0.0 copy-start.10
  65.8 0.9 shard_map.104
  66.8 28.4 %all_to_all.15 = bf16[16,32,128]{2,1,0:T(8,128)(2,1)S(1)} all-to-all(bf16[16,32,128]{2,1,0:T(8,128)(2,1)S(1)} %broadcast_in_dim.10), channel_id=1, replica_groups=mesh['zlo'=8,'x'=4,'zhi'=2,'y'=4,'core'=2] {'zhi','y','core'}, dimensions={0} | all-to-all | bytes 262144 | tf_op jit(solution)/shard_map/all_to_all | solution.py:224
  95.2 0.0 copy-done.2
  95.2 0.7 broadcast_in_dim.11
  95.9 9.3 %all-to-all-start.2 = ((bf16[32,32,128]{2,1,0:T(8,128)(2,1)}), bf16[32,32,128]{2,1,0:T(8,128)(2,1)S(1)}, u32[]{:S(2)}, u32[]{:S(2)}) async-start(bf16[32,32,128]{2,1,0:T(8,128)(2,1)} %broadcast_in_dim.11), calls=%async_computation.2 | async-start | bytes 524288 | tf_op jit(solution)/shard_map/all_to_all | solution.py:228
  105.2 0.0 copy-done.8
  105.2 0.0 copy-done.10
  105.2 0.1 copy.12.slot_ref
  105.3 0.6 pad_add_fusion.spot_ref
  105.9 0.1 pad_add_fusion.1.place_ref
  106.0 0.0 all-gather.7.cloned.1.call-done
  106.0 6.7 %shard_map.105 = (bf16[8,128,512]{2,1,0:T(8,128)(2,1)}, f32[128,128]{1,0:T(8,128)}) custom-call(s32[2]{0:T(128)} %pad_add_fusion.spot_ref, bf16[128,8192]{1,0:T(8,128)(2,1)} %x_ref.7, bf16[128,512]{1,0:T(8,128)(2,1)} %v_ref.5, bf16[8,144,512]{2,1,0:T(8,128)(2,1)} %copy-done.2, bf16[8,512,512]{2,1,0:T(8,128)(2,1)} %bitcast.18), custom_call_target="tpu_custom_call" | custom-call | flops 536870912 | bytes 4194304 | tf_op jit(solution)/shard_map/pallas_call | solution.py:232
  112.7 0.0 all-gather.5.cloned.1.call-done
  112.7 8.0 %shard_map.106 = bf16[128,8192]{1,0:T(8,128)(2,1)} custom-call(s32[2]{0:T(128)} %pad_add_fusion.spot_ref, bf16[128,8192]{1,0:T(8,128)(2,1)} %x_ref.7, bf16[128,512]{1,0:T(8,128)(2,1)} %v_ref.5, bf16[8,144,512]{2,1,0:T(8,128)(2,1)} %copy-done.2, bf16[8,512,512]{2,1,0:T(8,128)(2,1)} %bitcast.19, bf16[8,128,512]{2,1,0:T(8,128)(2,1)} %get-tuple-element.29.s_ref, ...), custom_call_target="tpu_custom_call" | custom-call | flops 536870912 | bytes 8388608 | tf_op jit(solution)/shard_map/pallas_call | solution.py:245
  120.8 2.5 %all-to-all-done.2.tab_ref = bf16[32,32,128]{2,1,0:T(8,128)(2,1)S(1)} async-done(((bf16[32,32,128]{2,1,0:T(8,128)(2,1)}), bf16[32,32,128]{2,1,0:T(8,128)(2,1)S(1)}, u32[]{:S(2)}, u32[]{:S(2)}) %all-to-all-start.2) | async-done | bytes 262176 | tf_op jit(solution)/shard_map/all_to_all | solution.py:228
  123.3 1.5 %shard_map.107 = (f32[128,256]{1,0:T(8,128)}, f32[2,32]{1,0:T(2,128)}) custom-call(s32[2]{0:T(128)S(1)} %pad_add_fusion.1.place_ref, bf16[32,32,128]{2,1,0:T(8,128)(2,1)S(1)} %all-to-all-done.2.tab_ref, f32[2,32,128]{2,1,0:T(8,128)S(1)} %bitcast.16, s32[32,1]{1,0:T(8,128)S(1)} %copy.12.slot_ref), custom_call_target="tpu_custom_call" | custom-call | tf_op jit(solution)/shard_map/pallas_call | solution.py:263
  (10 shorter events, 0.1 us)
Async XLA Ops:
  7.2 33.6 %copy-start.9 = (bf16[512]{0:T(512)(128)(2,1)S(1)}, bf16[512]{0:T(512)(128)(2,1)}, u32[]{:S(2)}) copy-start(bf16[512]{0:T(512)(128)(2,1)} %param.9) | copy-start | bytes 3076
  7.2 19.3 %copy-start.6 = (bf16[512,64]{0,1:T(8,128)(2,1)S(1)}, bf16[512,64]{0,1:T(8,128)(2,1)}, u32[]{:S(2)}) copy-start(bf16[512,64]{0,1:T(8,128)(2,1)} %param.12) | copy-start | bytes 196612
  7.2 98.8 %all-gather.7.cloned.1.call-start = ((), (), s32[]{:S(2)}) async-start(), calls=%async_computation.4 | async-start | bytes 4718592 | tf_op jit(solution)/shard_map/all_gather | solution.py:178
  10.4 30.3 %collective-permute-start = (bf16[208,512]{1,0:T(8,128)(2,1)S(1)}, bf16[208,512]{1,0:T(8,128)(2,1)S(1)}, u32[]{:S(2)}, u32[]{:S(2)}) collective-permute-start(bf16[208,512]{1,0:T(8,128)(2,1)S(1)} %pad_maximum_fusion.1), channel_id=1, source_target_pairs={{0,456},{8,448},{64,392},{72,384},{128,328},{136,320},{192,264},{2... | collective-permute-start | bytes 638984 | tf_op jit(solution)/shard_map/ppermute | solution.py:186
  22.5 1.6 %copy-start = (bf16[128,8192]{1,0:T(8,128)(2,1)S(1)}, bf16[128,8192]{1,0:T(8,128)(2,1)}, u32[]{:S(2)}) copy-start(bf16[128,8192]{1,0:T(8,128)(2,1)} %x_ref.7) | copy-start | bytes 6291460
  24.1 0.9 copy-start.3
  25.0 0.8 copy-start.5
  26.5 39.2 %copy-start.4 = (f32[128,128]{1,0:T(8,128)}, f32[128,128]{1,0:T(8,128)S(1)}, u32[]{:S(2)}) copy-start(f32[128,128]{1,0:T(8,128)S(1)} %get-tuple-element.23.inv_ref) | copy-start | bytes 196612
  40.7 0.7 copy-start.7
  42.5 23.2 %copy-start.1 = (bf16[128,8192]{1,0:T(8,128)(2,1)S(1)}, bf16[128,8192]{1,0:T(8,128)(2,1)}, u32[]{:S(2)}) copy-start(bf16[128,8192]{1,0:T(8,128)(2,1)} %x_ref.7) | copy-start | bytes 6291460
  42.5 23.2 %all-to-all-start = ((bf16[8,144,512]{2,1,0:T(8,128)(2,1)}), bf16[8,144,512]{2,1,0:T(8,128)(2,1)S(1)}, u32[]{:S(2)}, u32[]{:S(2)}) async-start(bf16[8,144,512]{2,1,0:T(8,128)(2,1)} %broadcast_in_dim.9), calls=%async_computation | async-start | bytes 2359296 | tf_op jit(solution)/shard_map/all_to_all | solution.py:205
  47.1 65.6 %all-gather.5.cloned.1.call-start = ((), (), s32[]{:S(2)}) async-start(), calls=%async_computation.3 | async-start | bytes 4718592 | tf_op jit(solution)/shard_map/all_gather | solution.py:214
  48.1 10.5 %collective-permute-start.1 = (bf16[128,512]{1,0:T(8,128)(2,1)S(1)}, bf16[128,512]{1,0:T(8,128)(2,1)S(1)}, u32[]{:S(2)}, u32[]{:S(2)}) collective-permute-start(bf16[128,512]{1,0:T(8,128)(2,1)S(1)} %slice.16), channel_id=1, source_target_pairs={{0,16},{16,32},{32,48},{48,0},{1,17},{17,33},{33,49},{49,1},{2,18}... | collective-permute-start | bytes 393224 | tf_op jit(solution)/shard_map/ppermute | solution.py:209
  51.5 9.7 %collective-permute-start.2 = (bf16[128,512]{1,0:T(8,128)(2,1)S(1)}, bf16[128,512]{1,0:T(8,128)(2,1)S(1)}, u32[]{:S(2)}, u32[]{:S(2)}) collective-permute-start(bf16[128,512]{1,0:T(8,128)(2,1)S(1)} %slice.16), channel_id=1, source_target_pairs={{0,32},{16,48},{32,0},{48,16},{1,33},{17,49},{33,1},{49,17},{2,34}... | collective-permute-start | bytes 393224 | tf_op jit(solution)/shard_map/ppermute | solution.py:209
  54.5 8.8 %collective-permute-start.3 = (bf16[128,512]{1,0:T(8,128)(2,1)S(1)}, bf16[128,512]{1,0:T(8,128)(2,1)S(1)}, u32[]{:S(2)}, u32[]{:S(2)}) collective-permute-start(bf16[128,512]{1,0:T(8,128)(2,1)S(1)} %slice.16), channel_id=1, source_target_pairs={{0,48},{16,0},{32,16},{48,32},{1,49},{17,1},{33,17},{49,33},{2,50}... | collective-permute-start | bytes 393224 | tf_op jit(solution)/shard_map/ppermute | solution.py:209
  65.7 29.5 %copy-start.2 = (bf16[8,144,512]{2,1,0:T(8,128)(2,1)}, bf16[8,144,512]{2,1,0:T(8,128)(2,1)S(1)}, u32[]{:S(2)}) copy-start(bf16[8,144,512]{2,1,0:T(8,128)(2,1)S(1)} %all-to-all-done.g_ref) | copy-start | bytes 3538948
  65.8 39.4 %copy-start.8 = (f32[2,4096]{1,0:T(2,128)S(1)}, f32[2,4096]{1,0:T(2,128)}, u32[]{:S(2)}) copy-start(f32[2,4096]{1,0:T(2,128)} %param.14) | copy-start | bytes 98308
  65.8 39.5 %copy-start.10 = (s32[32]{0:T(128)S(1)}, s32[32]{0:T(128)}, u32[]{:S(2)}) copy-start(s32[32]{0:T(128)} %param.15) | copy-start | bytes 388
  95.9 27.3 %all-to-all-start.2 = ((bf16[32,32,128]{2,1,0:T(8,128)(2,1)}), bf16[32,32,128]{2,1,0:T(8,128)(2,1)S(1)}, u32[]{:S(2)}, u32[]{:S(2)}) async-start(bf16[32,32,128]{2,1,0:T(8,128)(2,1)} %broadcast_in_dim.11), calls=%async_computation.2 | async-start | bytes 524288 | tf_op jit(solution)/shard_map/all_to_all | solution.py:228
Sparse Core Ops, SparseCore 0:
  10.2 46.7 all-gather.6
  65.9 40.9 all-gather.4

commit v4 on v3

--- a/solution.py
+++ b/solution.py
@@ -53,19 +53,21 @@
     ).astype(BF16)
 
 
-def partial_feats(zhi_ref, x_ref, g_ref, inv_ref, right_ref, out_ref, rows_ref):
-    near, both, depth = g_ref.shape
+def partial_feats(place_ref, x_ref, same_ref, other_ref, inv_ref, right_ref, out_ref, rows_ref):
+    chips, both, depth = same_ref.shape
     proj = (both - 16) // 2
-    zhi = zhi_ref[0]
+    zhi, core = place_ref[0], place_ref[1]
     acc = jnp.zeros((x_ref.shape[0], proj), F32)
     for half in range(2):
-        first = (zhi if half == 0 else 1 - zhi) * near
-        for at in range(near):
-            cols = pl.ds(pl.multiple_of((first + at) * depth, depth), depth)
-            acc = acc + lax.dot_general(
-                x_ref[:, cols], g_ref[at, half * proj : (half + 1) * proj, :], NT,
-                preferred_element_type=F32,
-            )
+        first = (zhi if half == 0 else 1 - zhi) * 2 * chips
+        for which, source in ((core, same_ref), (1 - core, other_ref)):
+            for at in range(chips):
+                start = (first + 2 * at + which) * depth
+                cols = pl.ds(pl.multiple_of(start, depth), depth)
+                acc = acc + lax.dot_general(
+                    x_ref[:, cols], source[at, half * proj : (half + 1) * proj, :], NT,
+                    preferred_element_type=F32,
+                )
     left = (acc * inv_ref[:, :1]).astype(BF16)
     rows_ref[...] = lax.dot_general(left, right_ref[...], TN, preferred_element_type=F32)
     even = rows_ref[pl.ds(0, proj // 2, stride=2), :]
@@ -202,25 +204,31 @@
     pair = jnp.concatenate(
         [folded(send), folded(recv), send[proj : proj + 8], recv[proj : proj + 8]], axis=0
     )
-    pairs = lax.all_to_all(
-        jnp.broadcast_to(pair[None], (near,) + pair.shape), NEAR, 0, 0, tiled=True
+    same = lax.all_to_all(
+        jnp.broadcast_to(pair[None], (near // 2,) + pair.shape), "y", 0, 0, tiled=True
     )
     moved = [rows_far] + [
         lax.ppermute(rows_far, "x", [(i, (i + hop) % across) for i in range(across)])
         for hop in range(1, across)
     ]
     shard_far = jnp.concatenate(moved, axis=0)
-    shard_far, pairs = lax.optimization_barrier((shard_far, pairs))
+    shard_far, same = lax.optimization_barrier((shard_far, same))
     weight_far = lax.all_gather(shard_far, NEAR, axis=0)
+    other = lax.ppermute(same, "core", [(0, 1), (1, 0)])
+    core = lax.axis_index("core")
+    gains = [part[:, 2 * proj :] for part in (same, other)]
+    first = [jnp.where(core == 0, gains[k], gains[1 - k]) for k in range(2)]
+    gains = jnp.stack(first, axis=1).reshape(near, 16, depth)
+    place_core = jnp.concatenate([zhi, core.astype(jnp.int32).reshape(1)])
 
     partial = pl.pallas_call(
         partial_feats,
         out_shape=shape((lines, 128), F32),
-        in_specs=[SMEM] + [VMEM] * 4,
+        in_specs=[SMEM] + [VMEM] * 5,
         out_specs=VMEM,
         scratch_shapes=[pltpu.VMEM((proj, proj), F32)],
         compiler_params=PARAMS,
-    )(zhi, hidden_in, pairs, inv, right)
+    )(place_core, hidden_in, same, other, inv, right)
     partials = lax.all_to_all(
         jnp.broadcast_to(partial.astype(BF16)[None], (group, lines, 128)), FSDP, 0, 0, tiled=True
     )
@@ -240,7 +248,7 @@
         ],
         compiler_params=LARGE,
         cost_estimate=cost(tokens * feats * width, feats * width),
-    )(spot, hidden_in, value_grad, pairs, weight_near)
+    )(spot, hidden_in, value_grad, gains, weight_near)
     weight_far, near_inner = lax.optimization_barrier((weight_far, near_inner))
     input_grad = pl.pallas_call(
         input_gradient,
@@ -256,7 +264,7 @@
         ],
         compiler_params=LARGE,
         cost_estimate=cost(tokens * feats * width, 2 * feats * width),
-    )(spot, hidden_in, value_grad, pairs, weight_far, near_scaled, near_inner, inv)
+    )(spot, hidden_in, value_grad, gains, weight_far, near_scaled, near_inner, inv)
 
     table, input_grad = lax.optimization_barrier((table, input_grad))
     place = jnp.stack([lax.axis_index(DP), lax.axis_index(FSDP)]).astype(jnp.int32)

time: 132 us -> 130 us (0.985)
  blocking collectives: 28.4 us -> 26.4 us
  waiting for transfers between devices: 23.7 us -> 21.8 us
  starting transfers between devices: 35.8 us -> 37.4 us
    all_to_all x1, blocking collectives: 28.4 us -> 26.4 us  [local(): lax.all_to_all(jnp.broadcast_to(partial.astype(BF16)[None], (group, lines...]
    ppermute x0 -> x1, starting transfers between devices: none -> 1.92 us  [local(): other = lax.ppermute(same, 'core', [(0, 1), (1, 0)])]
    ppermute x0 -> x1, waiting for transfers between devices: none -> 1.89 us  [local(): other = lax.ppermute(same, 'core', [(0, 1), (1, 0)])]
    all_to_all x1, waiting for transfers between devices: 1.58 us -> 0.01 us  [local(): lax.all_to_all(jnp.broadcast_to(pair[None], (near // 2,) + pair.shape), '...]
    unnamed x23 -> x15, local copies, waits for them, and re-layouts: 4 us -> 3.36 us
  transfers between devices with their start and end apart: 8 -> 9, of which waited for: 5 -> 5; matrix products, arithmetic and copies ran while one was open for 6% -> 7% of each run, Pallas kernels for 12% -> 13%
where the time goes in v4:
time: 130 us
  starting transfers between devices  37.4 us (29%)
  blocking collectives  26.4 us (20%)
  waiting for transfers between devices  21.8 us (17%)
  Pallas kernels  17.7 us (14%)
  between operations  14.3 us (11%)
  local copies, waits for them, and re-layouts  8.03 us (6%)
  other arithmetic  4.12 us (3%)
    all_to_all x1, blocking collectives, local(): lax.all_to_all(jnp.broadcast_to(partial.astype(BF16)[None], (group, lines...  26.4 us
    ppermute x1, waiting for transfers between devices, local(): recv = lax.ppermute(send, ('zlo', 'zhi'), mirror)  13.3 us
    ppermute x1, starting transfers between devices, local(): recv = lax.ppermute(send, ('zlo', 'zhi'), mirror)  11.4 us
    ppermute x3, starting transfers between devices, local(): lax.ppermute(rows_far, 'x', [(i, (i + hop) % across) for i in range(acros...  10.5 us
    all_to_all x1, starting transfers between devices, local(): lax.all_to_all(jnp.broadcast_to(own[None], (examples, lines, 128)), DP, 0...  9.05 us
    pallas_call x1, Pallas kernels, local(): pl.pallas_call(input_gradient, out_shape=shape((tokens, width), BF16), in...  7.71 us
    pallas_call x1, Pallas kernels, local(): pl.pallas_call(near_half, out_shape=(shape((near, tokens, depth), BF16),...  6.44 us
    all_to_all x1, starting transfers between devices, local(): lax.all_to_all(jnp.broadcast_to(pair[None], (near // 2,) + pair.shape), '...  4.46 us
  transfers between devices with their start and end apart: 9, of which 5 were waited for; matrix products, arithmetic and copies ran while one was open for 7% of the time, Pallas kernels for 13%

profile of v4, /device:TPU:2, one launch (start us, length us, event | category | flops | bytes accessed | tf_op | source)
XLA Modules:
  0.0 129.7 jit_solution(11302996083360544455)
XLA Ops:
  7.2 0.0 all-gather.7.cloned.1.call-start
  7.2 0.7 all-gather.7.cloned.1.call-update
  7.9 0.9 constant_dynamic-slice_fusion
  8.8 0.7 broadcast_in_dim.8
  9.5 0.9 pad_maximum_fusion.1
  10.4 11.4 %collective-permute-start = (bf16[208,512]{1,0:T(8,128)(2,1)S(1)}, bf16[208,512]{1,0:T(8,128)(2,1)S(1)}, u32[]{:S(2)}, u32[]{:S(2)}) collective-permute-start(bf16[208,512]{1,0:T(8,128)(2,1)S(1)} %pad_maximum_fusion.1), channel_id=1, source_target_pairs={{0,456},{8,448},{64,392},{72,384},{128,328},{136,320},{192,264},{2... | collective-permute-start | bytes 638984 | tf_op jit(solution)/shard_map/ppermute | solution.py:188
  21.8 0.7 convert_element_type.25
  22.5 0.0 copy-start
  22.5 1.6 %copy-done = bf16[128,8192]{1,0:T(8,128)(2,1)S(1)} copy-done((bf16[128,8192]{1,0:T(8,128)(2,1)S(1)}, bf16[128,8192]{1,0:T(8,128)(2,1)}, u32[]{:S(2)}) %copy-start) | copy-done | bytes 2097176
  24.1 0.0 copy-start.2
  24.1 0.9 copy-done.2
  25.0 0.0 copy-start.4
  25.0 0.8 copy-done.4
  25.8 0.0 copy-start.1
  25.8 0.7 shard_map.103
  26.5 0.0 copy-start.3
  26.5 0.9 multiply_convert_fusion.1
  27.4 13.3 %collective-permute-done = bf16[208,512]{1,0:T(8,128)(2,1)S(1)} collective-permute-done((bf16[208,512]{1,0:T(8,128)(2,1)S(1)}, bf16[208,512]{1,0:T(8,128)(2,1)S(1)}, u32[]{:S(2)}, u32[]{:S(2)}) %collective-permute-start) | collective-permute-done | bytes 213024 | tf_op jit(solution)/shard_map/ppermute | solution.py:188
  40.7 0.7 slice.25
  41.4 0.0 copy-start.5
  41.4 0.0 copy-start.6
  41.5 0.9 broadcast_in_dim.9
  42.3 4.5 %all-to-all-start = ((bf16[4,144,512]{2,1,0:T(8,128)(2,1)}), bf16[4,144,512]{2,1,0:T(8,128)(2,1)S(1)}, u32[]{:S(2)}, u32[]{:S(2)}) async-start(bf16[4,144,512]{2,1,0:T(8,128)(2,1)} %broadcast_in_dim.9), calls=%async_computation | async-start | bytes 1179648 | tf_op jit(solution)/shard_map/all_to_all | solution.py:207
  46.8 0.0 all-gather.5.cloned.1.call-start
  46.8 3.4 %collective-permute-start.1 = (bf16[128,512]{1,0:T(8,128)(2,1)S(1)}, bf16[128,512]{1,0:T(8,128)(2,1)S(1)}, u32[]{:S(2)}, u32[]{:S(2)}) collective-permute-start(bf16[128,512]{1,0:T(8,128)(2,1)S(1)} %slice.22), channel_id=1, source_target_pairs={{0,16},{16,32},{32,48},{48,0},{1,17},{17,33},{33,49},{49,1},{2,18}... | collective-permute-start | bytes 393224 | tf_op jit(solution)/shard_map/ppermute | solution.py:211
  50.2 3.0 %collective-permute-start.2 = (bf16[128,512]{1,0:T(8,128)(2,1)S(1)}, bf16[128,512]{1,0:T(8,128)(2,1)S(1)}, u32[]{:S(2)}, u32[]{:S(2)}) collective-permute-start(bf16[128,512]{1,0:T(8,128)(2,1)S(1)} %slice.22), channel_id=1, source_target_pairs={{0,32},{16,48},{32,0},{48,16},{1,33},{17,49},{33,1},{49,17},{2,34}... | collective-permute-start | bytes 393224 | tf_op jit(solution)/shard_map/ppermute | solution.py:211
  53.2 4.1 %collective-permute-start.3 = (bf16[128,512]{1,0:T(8,128)(2,1)S(1)}, bf16[128,512]{1,0:T(8,128)(2,1)S(1)}, u32[]{:S(2)}, u32[]{:S(2)}) collective-permute-start(bf16[128,512]{1,0:T(8,128)(2,1)S(1)} %slice.22), channel_id=1, source_target_pairs={{0,48},{16,0},{32,16},{48,32},{1,49},{17,1},{33,17},{49,33},{2,50}... | collective-permute-start | bytes 393224 | tf_op jit(solution)/shard_map/ppermute | solution.py:211
  57.3 0.0 collective-permute-done.1
  57.3 2.7 %collective-permute-done.2 = bf16[128,512]{1,0:T(8,128)(2,1)S(1)} collective-permute-done((bf16[128,512]{1,0:T(8,128)(2,1)S(1)}, bf16[128,512]{1,0:T(8,128)(2,1)S(1)}, u32[]{:S(2)}, u32[]{:S(2)}) %collective-permute-start.2) | collective-permute-done | bytes 131104 | tf_op jit(solution)/shard_map/ppermute | solution.py:211
  60.0 0.9 collective-permute-done.3
  60.8 0.8 pad_maximum_fusion
  61.7 0.0 all-to-all-done.same_ref
  61.7 0.0 all-gather.5.cloned.1.call-update
  61.7 1.9 %collective-permute-start.4 = (bf16[4,144,512]{2,1,0:T(8,128)(2,1)S(1)}, bf16[4,144,512]{2,1,0:T(8,128)(2,1)S(1)}, u32[]{:S(2)}, u32[]{:S(2)}) collective-permute-start(bf16[4,144,512]{2,1,0:T(8,128)(2,1)S(1)} %all-to-all-done.same_ref), channel_id=1, source_target_pairs={{0,1},{1,0},{2,3},{3,2},{4,5},{5,4},{6,7},{7,6},{8,9},{9,8},{10,11... | collective-permute-start | bytes 1769480 | tf_op jit(solution)/shard_map/ppermute | solution.py:217
  63.6 0.1 pad_add_fusion.place_ref
  63.7 1.9 %collective-permute-done.4.other_ref = bf16[4,144,512]{2,1,0:T(8,128)(2,1)S(1)} collective-permute-done((bf16[4,144,512]{2,1,0:T(8,128)(2,1)S(1)}, bf16[4,144,512]{2,1,0:T(8,128)(2,1)S(1)}, u32[]{:S(2)}, u32[]{:S(2)}) %collective-permute-start.4) | collective-permute-done | bytes 589856 | tf_op jit(solution)/shard_map/ppermute | solution.py:217
  65.6 0.0 copy-done.1
  65.6 1.5 %shard_map.104 = f32[32,128]{1,0:T(8,128)S(1)} custom-call(s32[2]{0:T(128)S(1)} %pad_add_fusion.place_ref, bf16[128,8192]{1,0:T(8,128)(2,1)S(1)} %copy-done.1, bf16[4,144,512]{2,1,0:T(8,128)(2,1)S(1)} %all-to-all-done.same_ref, bf16[4,144,512]{2,1,0:T(8,128)(2,1)S(1)} %collective-permute-done.4.other_ref, f32[128,128]{1,0:T(8,128)S(1)} %get-tuple-element.23.inv_ref, ...), custom_call_target="tpu_custom_call" | custom-call | tf_op jit(solution)/shard_map/pallas_call | solution.py:224
  67.1 26.4 %all_to_all.15 = bf16[16,32,128]{2,1,0:T(8,128)(2,1)S(1)} all-to-all(bf16[16,32,128]{2,1,0:T(8,128)(2,1)S(1)} %broadcast_in_dim.10), channel_id=1, replica_groups=mesh['zlo'=8,'x'=4,'zhi'=2,'y'=4,'core'=2] {'zhi','y','core'}, dimensions={0} | all-to-all | bytes 262144 | tf_op jit(solution)/shard_map/all_to_all | solution.py:232
  93.6 0.7 broadcast_in_dim.11
  94.3 0.0 copy-done.3
  94.3 9.0 %all-to-all-start.2 = ((bf16[32,32,128]{2,1,0:T(8,128)(2,1)}), bf16[32,32,128]{2,1,0:T(8,128)(2,1)S(1)}, u32[]{:S(2)}, u32[]{:S(2)}) async-start(bf16[32,32,128]{2,1,0:T(8,128)(2,1)} %broadcast_in_dim.11), calls=%async_computation.2 | async-start | bytes 524288 | tf_op jit(solution)/shard_map/all_to_all | solution.py:236
  103.4 0.0 copy-done.5
  103.4 0.0 copy-done.6
  103.4 0.1 copy.14.slot_ref
  103.5 0.6 pad_add_fusion.1.spot_ref
  104.1 0.1 pad_add_fusion.2.place_ref
  104.3 0.7 copy.13
  104.9 0.0 all-gather.7.cloned.1.call-done
  104.9 6.4 %shard_map.105 = (bf16[8,128,512]{2,1,0:T(8,128)(2,1)}, f32[128,128]{1,0:T(8,128)}) custom-call(s32[2]{0:T(128)} %pad_add_fusion.1.spot_ref, bf16[128,8192]{1,0:T(8,128)(2,1)} %x_ref.7, bf16[128,512]{1,0:T(8,128)(2,1)} %v_ref.5, bf16[8,16,512]{2,1,0:T(8,128)(2,1)} %bitcast.26, bf16[8,512,512]{2,1,0:T(8,128)(2,1)} %bitcast.25), custom_call_target="tpu_custom_call" | custom-call | flops 536870912 | bytes 4194304 | tf_op jit(solution)/shard_map/pallas_call | solution.py:240
  111.4 0.0 all-gather.5.cloned.1.call-done
  111.4 7.7 %shard_map.106 = bf16[128,8192]{1,0:T(8,128)(2,1)} custom-call(s32[2]{0:T(128)} %pad_add_fusion.1.spot_ref, bf16[128,8192]{1,0:T(8,128)(2,1)} %x_ref.7, bf16[128,512]{1,0:T(8,128)(2,1)} %v_ref.5, bf16[8,16,512]{2,1,0:T(8,128)(2,1)} %bitcast.27, bf16[8,512,512]{2,1,0:T(8,128)(2,1)} %bitcast.24, bf16[8,128,512]{2,1,0:T(8,128)(2,1)} %get-tuple-element.29.s_ref, ...), custom_call_target="tpu_custom_call" | custom-call | flops 536870912 | bytes 8388608 | tf_op jit(solution)/shard_map/pallas_call | solution.py:253
  119.1 2.3 %all-to-all-done.2.tab_ref = bf16[32,32,128]{2,1,0:T(8,128)(2,1)S(1)} async-done(((bf16[32,32,128]{2,1,0:T(8,128)(2,1)}), bf16[32,32,128]{2,1,0:T(8,128)(2,1)S(1)}, u32[]{:S(2)}, u32[]{:S(2)}) %all-to-all-start.2) | async-done | bytes 262176 | tf_op jit(solution)/shard_map/all_to_all | solution.py:236
  121.5 1.5 %shard_map.107 = (f32[128,256]{1,0:T(8,128)}, f32[2,32]{1,0:T(2,128)}) custom-call(s32[2]{0:T(128)S(1)} %pad_add_fusion.2.place_ref, bf16[32,32,128]{2,1,0:T(8,128)(2,1)S(1)} %all-to-all-done.2.tab_ref, f32[2,32,128]{2,1,0:T(8,128)S(1)} %bitcast.22, s32[32,1]{1,0:T(8,128)S(1)} %copy.14.slot_ref), custom_call_target="tpu_custom_call" | custom-call | tf_op jit(solution)/shard_map/pallas_call | solution.py:271
  (11 shorter events, 0.1 us)
Async XLA Ops:
  7.2 97.8 %all-gather.7.cloned.1.call-start = ((), (), s32[]{:S(2)}) async-start(), calls=%async_computation.4 | async-start | bytes 4718592 | tf_op jit(solution)/shard_map/all_gather | solution.py:180
  10.4 30.3 %collective-permute-start = (bf16[208,512]{1,0:T(8,128)(2,1)S(1)}, bf16[208,512]{1,0:T(8,128)(2,1)S(1)}, u32[]{:S(2)}, u32[]{:S(2)}) collective-permute-start(bf16[208,512]{1,0:T(8,128)(2,1)S(1)} %pad_maximum_fusion.1), channel_id=1, source_target_pairs={{0,456},{8,448},{64,392},{72,384},{128,328},{136,320},{192,264},{2... | collective-permute-start | bytes 638984 | tf_op jit(solution)/shard_map/ppermute | solution.py:188
  22.5 1.6 %copy-start = (bf16[128,8192]{1,0:T(8,128)(2,1)S(1)}, bf16[128,8192]{1,0:T(8,128)(2,1)}, u32[]{:S(2)}) copy-start(bf16[128,8192]{1,0:T(8,128)(2,1)} %x_ref.7) | copy-start | bytes 6291460
  24.1 0.9 copy-start.2
  25.0 0.8 copy-start.4
  25.8 39.8 %copy-start.1 = (bf16[128,8192]{1,0:T(8,128)(2,1)S(1)}, bf16[128,8192]{1,0:T(8,128)(2,1)}, u32[]{:S(2)}) copy-start(bf16[128,8192]{1,0:T(8,128)(2,1)} %x_ref.7) | copy-start | bytes 6291460
  26.5 67.9 %copy-start.3 = (f32[128,128]{1,0:T(8,128)}, f32[128,128]{1,0:T(8,128)S(1)}, u32[]{:S(2)}) copy-start(f32[128,128]{1,0:T(8,128)S(1)} %get-tuple-element.23.inv_ref) | copy-start | bytes 196612
  41.4 62.0 %copy-start.5 = (f32[2,4096]{1,0:T(2,128)S(1)}, f32[2,4096]{1,0:T(2,128)}, u32[]{:S(2)}) copy-start(f32[2,4096]{1,0:T(2,128)} %param.14) | copy-start | bytes 98308
  41.4 62.0 %copy-start.6 = (s32[32]{0:T(128)S(1)}, s32[32]{0:T(128)}, u32[]{:S(2)}) copy-start(s32[32]{0:T(128)} %param.15) | copy-start | bytes 388
  42.3 19.4 %all-to-all-start = ((bf16[4,144,512]{2,1,0:T(8,128)(2,1)}), bf16[4,144,512]{2,1,0:T(8,128)(2,1)S(1)}, u32[]{:S(2)}, u32[]{:S(2)}) async-start(bf16[4,144,512]{2,1,0:T(8,128)(2,1)} %broadcast_in_dim.9), calls=%async_computation | async-start | bytes 1179648 | tf_op jit(solution)/shard_map/all_to_all | solution.py:207
  46.8 64.6 %all-gather.5.cloned.1.call-start = ((), (), s32[]{:S(2)}) async-start(), calls=%async_computation.3 | async-start | bytes 4718592 | tf_op jit(solution)/shard_map/all_gather | solution.py:216
  46.8 10.5 %collective-permute-start.1 = (bf16[128,512]{1,0:T(8,128)(2,1)S(1)}, bf16[128,512]{1,0:T(8,128)(2,1)S(1)}, u32[]{:S(2)}, u32[]{:S(2)}) collective-permute-start(bf16[128,512]{1,0:T(8,128)(2,1)S(1)} %slice.22), channel_id=1, source_target_pairs={{0,16},{16,32},{32,48},{48,0},{1,17},{17,33},{33,49},{49,1},{2,18}... | collective-permute-start | bytes 393224 | tf_op jit(solution)/shard_map/ppermute | solution.py:211
  50.2 9.8 %collective-permute-start.2 = (bf16[128,512]{1,0:T(8,128)(2,1)S(1)}, bf16[128,512]{1,0:T(8,128)(2,1)S(1)}, u32[]{:S(2)}, u32[]{:S(2)}) collective-permute-start(bf16[128,512]{1,0:T(8,128)(2,1)S(1)} %slice.22), channel_id=1, source_target_pairs={{0,32},{16,48},{32,0},{48,16},{1,33},{17,49},{33,1},{49,17},{2,34}... | collective-permute-start | bytes 393224 | tf_op jit(solution)/shard_map/ppermute | solution.py:211
  53.2 7.6 %collective-permute-start.3 = (bf16[128,512]{1,0:T(8,128)(2,1)S(1)}, bf16[128,512]{1,0:T(8,128)(2,1)S(1)}, u32[]{:S(2)}, u32[]{:S(2)}) collective-permute-start(bf16[128,512]{1,0:T(8,128)(2,1)S(1)} %slice.22), channel_id=1, source_target_pairs={{0,48},{16,0},{32,16},{48,32},{1,49},{17,1},{33,17},{49,33},{2,50}... | collective-permute-start | bytes 393224 | tf_op jit(solution)/shard_map/ppermute | solution.py:211
  61.7 3.9 %collective-permute-start.4 = (bf16[4,144,512]{2,1,0:T(8,128)(2,1)S(1)}, bf16[4,144,512]{2,1,0:T(8,128)(2,1)S(1)}, u32[]{:S(2)}, u32[]{:S(2)}) collective-permute-start(bf16[4,144,512]{2,1,0:T(8,128)(2,1)S(1)} %all-to-all-done.same_ref), channel_id=1, source_target_pairs={{0,1},{1,0},{2,3},{3,2},{4,5},{5,4},{6,7},{7,6},{8,9},{9,8},{10,11... | collective-permute-start | bytes 1769480 | tf_op jit(solution)/shard_map/ppermute | solution.py:217
  94.3 27.1 %all-to-all-start.2 = ((bf16[32,32,128]{2,1,0:T(8,128)(2,1)}), bf16[32,32,128]{2,1,0:T(8,128)(2,1)S(1)}, u32[]{:S(2)}, u32[]{:S(2)}) async-start(bf16[32,32,128]{2,1,0:T(8,128)(2,1)} %broadcast_in_dim.11), calls=%async_computation.2 | async-start | bytes 524288 | tf_op jit(solution)/shard_map/all_to_all | solution.py:236
Sparse Core Ops, SparseCore 0:
  10.2 46.6 all-gather.6
  61.8 41.4 all-gather.4

commit v5 on v4

--- a/solution.py
+++ b/solution.py
@@ -212,7 +212,7 @@
         for hop in range(1, across)
     ]
     shard_far = jnp.concatenate(moved, axis=0)
-    shard_far, same = lax.optimization_barrier((shard_far, same))
+    shard_far, _ = lax.optimization_barrier((shard_far, same))
     weight_far = lax.all_gather(shard_far, NEAR, axis=0)
     other = lax.ppermute(same, "core", [(0, 1), (1, 0)])
     core = lax.axis_index("core")

time: 130 us -> 130 us (level)
  no operation moved by 1% of the time
where the time goes in v5:
time: 130 us
  starting transfers between devices  37.4 us (29%)
  blocking collectives  26.4 us (20%)
  waiting for transfers between devices  21.8 us (17%)
  Pallas kernels  17.7 us (14%)
  between operations  14.3 us (11%)
  local copies, waits for them, and re-layouts  8.03 us (6%)
  other arithmetic  4.12 us (3%)
    all_to_all x1, blocking collectives, local(): lax.all_to_all(jnp.broadcast_to(partial.astype(BF16)[None], (group, lines...  26.4 us
    ppermute x1, waiting for transfers between devices, local(): recv = lax.ppermute(send, ('zlo', 'zhi'), mirror)  13.3 us
    ppermute x1, starting transfers between devices, local(): recv = lax.ppermute(send, ('zlo', 'zhi'), mirror)  11.4 us
    ppermute x3, starting transfers between devices, local(): lax.ppermute(rows_far, 'x', [(i, (i + hop) % across) for i in range(acros...  10.5 us
    all_to_all x1, starting transfers between devices, local(): lax.all_to_all(jnp.broadcast_to(own[None], (examples, lines, 128)), DP, 0...  9.05 us
    pallas_call x1, Pallas kernels, local(): pl.pallas_call(input_gradient, out_shape=shape((tokens, width), BF16), in...  7.71 us
    pallas_call x1, Pallas kernels, local(): pl.pallas_call(near_half, out_shape=(shape((near, tokens, depth), BF16),...  6.44 us
    all_to_all x1, starting transfers between devices, local(): lax.all_to_all(jnp.broadcast_to(pair[None], (near // 2,) + pair.shape), '...  4.46 us
  transfers between devices with their start and end apart: 9, of which 5 were waited for; matrix products, arithmetic and copies ran while one was open for 7% of the time, Pallas kernels for 13%

profile of v5, /device:TPU:2, one launch (start us, length us, event | category | flops | bytes accessed | tf_op | source)
XLA Modules:
  0.0 129.7 jit_solution(11302996083360544455)
XLA Ops:
  7.2 0.0 all-gather.7.cloned.1.call-start
  7.2 0.7 all-gather.7.cloned.1.call-update
  7.9 0.9 constant_dynamic-slice_fusion
  8.8 0.7 broadcast_in_dim.8
  9.5 0.9 pad_maximum_fusion.1
  10.4 11.4 %collective-permute-start = (bf16[208,512]{1,0:T(8,128)(2,1)S(1)}, bf16[208,512]{1,0:T(8,128)(2,1)S(1)}, u32[]{:S(2)}, u32[]{:S(2)}) collective-permute-start(bf16[208,512]{1,0:T(8,128)(2,1)S(1)} %pad_maximum_fusion.1), channel_id=1, source_target_pairs={{0,456},{8,448},{64,392},{72,384},{128,328},{136,320},{192,264},{2... | collective-permute-start | bytes 638984 | tf_op jit(solution)/shard_map/ppermute | solution.py:188
  21.8 0.7 convert_element_type.25
  22.5 0.0 copy-start
  22.5 1.6 %copy-done = bf16[128,8192]{1,0:T(8,128)(2,1)S(1)} copy-done((bf16[128,8192]{1,0:T(8,128)(2,1)S(1)}, bf16[128,8192]{1,0:T(8,128)(2,1)}, u32[]{:S(2)}) %copy-start) | copy-done | bytes 2097176
  24.1 0.0 copy-start.2
  24.1 0.9 copy-done.2
  25.0 0.0 copy-start.4
  25.0 0.8 copy-done.4
  25.8 0.0 copy-start.1
  25.8 0.7 shard_map.103
  26.5 0.0 copy-start.3
  26.5 0.9 multiply_convert_fusion.1
  27.4 13.3 %collective-permute-done = bf16[208,512]{1,0:T(8,128)(2,1)S(1)} collective-permute-done((bf16[208,512]{1,0:T(8,128)(2,1)S(1)}, bf16[208,512]{1,0:T(8,128)(2,1)S(1)}, u32[]{:S(2)}, u32[]{:S(2)}) %collective-permute-start) | collective-permute-done | bytes 213024 | tf_op jit(solution)/shard_map/ppermute | solution.py:188
  40.7 0.7 slice.24
  41.4 0.0 copy-start.5
  41.4 0.0 copy-start.6
  41.5 0.9 broadcast_in_dim.9
  42.3 4.5 %all-to-all-start = ((bf16[4,144,512]{2,1,0:T(8,128)(2,1)}), bf16[4,144,512]{2,1,0:T(8,128)(2,1)S(1)}, u32[]{:S(2)}, u32[]{:S(2)}) async-start(bf16[4,144,512]{2,1,0:T(8,128)(2,1)} %broadcast_in_dim.9), calls=%async_computation | async-start | bytes 1179648 | tf_op jit(solution)/shard_map/all_to_all | solution.py:207
  46.8 0.0 all-gather.5.cloned.1.call-start
  46.8 3.4 %collective-permute-start.2 = (bf16[128,512]{1,0:T(8,128)(2,1)S(1)}, bf16[128,512]{1,0:T(8,128)(2,1)S(1)}, u32[]{:S(2)}, u32[]{:S(2)}) collective-permute-start(bf16[128,512]{1,0:T(8,128)(2,1)S(1)} %slice.28), channel_id=1, source_target_pairs={{0,16},{16,32},{32,48},{48,0},{1,17},{17,33},{33,49},{49,1},{2,18}... | collective-permute-start | bytes 393224 | tf_op jit(solution)/shard_map/ppermute | solution.py:211
  50.2 3.0 %collective-permute-start.3 = (bf16[128,512]{1,0:T(8,128)(2,1)S(1)}, bf16[128,512]{1,0:T(8,128)(2,1)S(1)}, u32[]{:S(2)}, u32[]{:S(2)}) collective-permute-start(bf16[128,512]{1,0:T(8,128)(2,1)S(1)} %slice.28), channel_id=1, source_target_pairs={{0,32},{16,48},{32,0},{48,16},{1,33},{17,49},{33,1},{49,17},{2,34}... | collective-permute-start | bytes 393224 | tf_op jit(solution)/shard_map/ppermute | solution.py:211
  53.2 4.1 %collective-permute-start.4 = (bf16[128,512]{1,0:T(8,128)(2,1)S(1)}, bf16[128,512]{1,0:T(8,128)(2,1)S(1)}, u32[]{:S(2)}, u32[]{:S(2)}) collective-permute-start(bf16[128,512]{1,0:T(8,128)(2,1)S(1)} %slice.28), channel_id=1, source_target_pairs={{0,48},{16,0},{32,16},{48,32},{1,49},{17,1},{33,17},{49,33},{2,50}... | collective-permute-start | bytes 393224 | tf_op jit(solution)/shard_map/ppermute | solution.py:211
  57.3 0.0 collective-permute-done.2
  57.3 2.7 %collective-permute-done.3 = bf16[128,512]{1,0:T(8,128)(2,1)S(1)} collective-permute-done((bf16[128,512]{1,0:T(8,128)(2,1)S(1)}, bf16[128,512]{1,0:T(8,128)(2,1)S(1)}, u32[]{:S(2)}, u32[]{:S(2)}) %collective-permute-start.3) | collective-permute-done | bytes 131104 | tf_op jit(solution)/shard_map/ppermute | solution.py:211
  60.0 0.9 collective-permute-done.4
  60.8 0.8 pad_maximum_fusion
  61.7 0.0 all-to-all-done.same_ref
  61.7 0.0 all-gather.5.cloned.1.call-update
  61.7 1.9 %collective-permute-start.1 = (bf16[4,144,512]{2,1,0:T(8,128)(2,1)S(1)}, bf16[4,144,512]{2,1,0:T(8,128)(2,1)S(1)}, u32[]{:S(2)}, u32[]{:S(2)}) collective-permute-start(bf16[4,144,512]{2,1,0:T(8,128)(2,1)S(1)} %all-to-all-done.same_ref), channel_id=1, source_target_pairs={{0,1},{1,0},{2,3},{3,2},{4,5},{5,4},{6,7},{7,6},{8,9},{9,8},{10,11... | collective-permute-start | bytes 1769480 | tf_op jit(solution)/shard_map/ppermute | solution.py:217
  63.6 0.1 pad_add_fusion.place_ref
  63.7 1.9 %collective-permute-done.1.other_ref = bf16[4,144,512]{2,1,0:T(8,128)(2,1)S(1)} collective-permute-done((bf16[4,144,512]{2,1,0:T(8,128)(2,1)S(1)}, bf16[4,144,512]{2,1,0:T(8,128)(2,1)S(1)}, u32[]{:S(2)}, u32[]{:S(2)}) %collective-permute-start.1) | collective-permute-done | bytes 589856 | tf_op jit(solution)/shard_map/ppermute | solution.py:217
  65.6 0.0 copy-done.1
  65.6 1.5 %shard_map.104 = f32[32,128]{1,0:T(8,128)S(1)} custom-call(s32[2]{0:T(128)S(1)} %pad_add_fusion.place_ref, bf16[128,8192]{1,0:T(8,128)(2,1)S(1)} %copy-done.1, bf16[4,144,512]{2,1,0:T(8,128)(2,1)S(1)} %all-to-all-done.same_ref, bf16[4,144,512]{2,1,0:T(8,128)(2,1)S(1)} %collective-permute-done.1.other_ref, f32[128,128]{1,0:T(8,128)S(1)} %get-tuple-element.21.inv_ref, ...), custom_call_target="tpu_custom_call" | custom-call | tf_op jit(solution)/shard_map/pallas_call | solution.py:224
  67.1 26.4 %all_to_all.15 = bf16[16,32,128]{2,1,0:T(8,128)(2,1)S(1)} all-to-all(bf16[16,32,128]{2,1,0:T(8,128)(2,1)S(1)} %broadcast_in_dim.10), channel_id=1, replica_groups=mesh['zlo'=8,'x'=4,'zhi'=2,'y'=4,'core'=2] {'zhi','y','core'}, dimensions={0} | all-to-all | bytes 262144 | tf_op jit(solution)/shard_map/all_to_all | solution.py:232
  93.6 0.7 broadcast_in_dim.11
  94.3 0.0 copy-done.3
  94.3 9.0 %all-to-all-start.2 = ((bf16[32,32,128]{2,1,0:T(8,128)(2,1)}), bf16[32,32,128]{2,1,0:T(8,128)(2,1)S(1)}, u32[]{:S(2)}, u32[]{:S(2)}) async-start(bf16[32,32,128]{2,1,0:T(8,128)(2,1)} %broadcast_in_dim.11), calls=%async_computation.2 | async-start | bytes 524288 | tf_op jit(solution)/shard_map/all_to_all | solution.py:236
  103.4 0.0 copy-done.5
  103.4 0.0 copy-done.6
  103.4 0.1 copy.14.slot_ref
  103.5 0.6 pad_add_fusion.1.spot_ref
  104.1 0.1 pad_add_fusion.2.place_ref
  104.3 0.7 copy.13
  104.9 0.0 all-gather.7.cloned.1.call-done
  104.9 6.4 %shard_map.105 = (bf16[8,128,512]{2,1,0:T(8,128)(2,1)}, f32[128,128]{1,0:T(8,128)}) custom-call(s32[2]{0:T(128)} %pad_add_fusion.1.spot_ref, bf16[128,8192]{1,0:T(8,128)(2,1)} %x_ref.7, bf16[128,512]{1,0:T(8,128)(2,1)} %v_ref.5, bf16[8,16,512]{2,1,0:T(8,128)(2,1)} %bitcast.26, bf16[8,512,512]{2,1,0:T(8,128)(2,1)} %bitcast.25), custom_call_target="tpu_custom_call" | custom-call | flops 536870912 | bytes 4194304 | tf_op jit(solution)/shard_map/pallas_call | solution.py:240
  111.4 0.0 all-gather.5.cloned.1.call-done
  111.4 7.7 %shard_map.106 = bf16[128,8192]{1,0:T(8,128)(2,1)} custom-call(s32[2]{0:T(128)} %pad_add_fusion.1.spot_ref, bf16[128,8192]{1,0:T(8,128)(2,1)} %x_ref.7, bf16[128,512]{1,0:T(8,128)(2,1)} %v_ref.5, bf16[8,16,512]{2,1,0:T(8,128)(2,1)} %bitcast.27, bf16[8,512,512]{2,1,0:T(8,128)(2,1)} %bitcast.24, bf16[8,128,512]{2,1,0:T(8,128)(2,1)} %get-tuple-element.27.s_ref, ...), custom_call_target="tpu_custom_call" | custom-call | flops 536870912 | bytes 8388608 | tf_op jit(solution)/shard_map/pallas_call | solution.py:253
  119.1 2.3 %all-to-all-done.2.tab_ref = bf16[32,32,128]{2,1,0:T(8,128)(2,1)S(1)} async-done(((bf16[32,32,128]{2,1,0:T(8,128)(2,1)}), bf16[32,32,128]{2,1,0:T(8,128)(2,1)S(1)}, u32[]{:S(2)}, u32[]{:S(2)}) %all-to-all-start.2) | async-done | bytes 262176 | tf_op jit(solution)/shard_map/all_to_all | solution.py:236
  121.5 1.5 %shard_map.107 = (f32[128,256]{1,0:T(8,128)}, f32[2,32]{1,0:T(2,128)}) custom-call(s32[2]{0:T(128)S(1)} %pad_add_fusion.2.place_ref, bf16[32,32,128]{2,1,0:T(8,128)(2,1)S(1)} %all-to-all-done.2.tab_ref, f32[2,32,128]{2,1,0:T(8,128)S(1)} %bitcast.22, s32[32,1]{1,0:T(8,128)S(1)} %copy.14.slot_ref), custom_call_target="tpu_custom_call" | custom-call | tf_op jit(solution)/shard_map/pallas_call | solution.py:271
  (11 shorter events, 0.1 us)
Async XLA Ops:
  7.2 97.8 %all-gather.7.cloned.1.call-start = ((), (), s32[]{:S(2)}) async-start(), calls=%async_computation.4 | async-start | bytes 4718592 | tf_op jit(solution)/shard_map/all_gather | solution.py:180
  10.4 30.3 %collective-permute-start = (bf16[208,512]{1,0:T(8,128)(2,1)S(1)}, bf16[208,512]{1,0:T(8,128)(2,1)S(1)}, u32[]{:S(2)}, u32[]{:S(2)}) collective-permute-start(bf16[208,512]{1,0:T(8,128)(2,1)S(1)} %pad_maximum_fusion.1), channel_id=1, source_target_pairs={{0,456},{8,448},{64,392},{72,384},{128,328},{136,320},{192,264},{2... | collective-permute-start | bytes 638984 | tf_op jit(solution)/shard_map/ppermute | solution.py:188
  22.5 1.6 %copy-start = (bf16[128,8192]{1,0:T(8,128)(2,1)S(1)}, bf16[128,8192]{1,0:T(8,128)(2,1)}, u32[]{:S(2)}) copy-start(bf16[128,8192]{1,0:T(8,128)(2,1)} %x_ref.7) | copy-start | bytes 6291460
  24.1 0.9 copy-start.2
  25.0 0.8 copy-start.4
  25.8 39.8 %copy-start.1 = (bf16[128,8192]{1,0:T(8,128)(2,1)S(1)}, bf16[128,8192]{1,0:T(8,128)(2,1)}, u32[]{:S(2)}) copy-start(bf16[128,8192]{1,0:T(8,128)(2,1)} %x_ref.7) | copy-start | bytes 6291460
  26.5 67.9 %copy-start.3 = (f32[128,128]{1,0:T(8,128)}, f32[128,128]{1,0:T(8,128)S(1)}, u32[]{:S(2)}) copy-start(f32[128,128]{1,0:T(8,128)S(1)} %get-tuple-element.21.inv_ref) | copy-start | bytes 196612
  41.4 62.0 %copy-start.5 = (f32[2,4096]{1,0:T(2,128)S(1)}, f32[2,4096]{1,0:T(2,128)}, u32[]{:S(2)}) copy-start(f32[2,4096]{1,0:T(2,128)} %param.14) | copy-start | bytes 98308
  41.4 62.0 %copy-start.6 = (s32[32]{0:T(128)S(1)}, s32[32]{0:T(128)}, u32[]{:S(2)}) copy-start(s32[32]{0:T(128)} %param.15) | copy-start | bytes 388
  42.3 19.4 %all-to-all-start = ((bf16[4,144,512]{2,1,0:T(8,128)(2,1)}), bf16[4,144,512]{2,1,0:T(8,128)(2,1)S(1)}, u32[]{:S(2)}, u32[]{:S(2)}) async-start(bf16[4,144,512]{2,1,0:T(8,128)(2,1)} %broadcast_in_dim.9), calls=%async_computation | async-start | bytes 1179648 | tf_op jit(solution)/shard_map/all_to_all | solution.py:207
  46.8 64.6 %all-gather.5.cloned.1.call-start = ((), (), s32[]{:S(2)}) async-start(), calls=%async_computation.3 | async-start | bytes 4718592 | tf_op jit(solution)/shard_map/all_gather | solution.py:216
  46.8 10.5 %collective-permute-start.2 = (bf16[128,512]{1,0:T(8,128)(2,1)S(1)}, bf16[128,512]{1,0:T(8,128)(2,1)S(1)}, u32[]{:S(2)}, u32[]{:S(2)}) collective-permute-start(bf16[128,512]{1,0:T(8,128)(2,1)S(1)} %slice.28), channel_id=1, source_target_pairs={{0,16},{16,32},{32,48},{48,0},{1,17},{17,33},{33,49},{49,1},{2,18}... | collective-permute-start | bytes 393224 | tf_op jit(solution)/shard_map/ppermute | solution.py:211
  50.2 9.8 %collective-permute-start.3 = (bf16[128,512]{1,0:T(8,128)(2,1)S(1)}, bf16[128,512]{1,0:T(8,128)(2,1)S(1)}, u32[]{:S(2)}, u32[]{:S(2)}) collective-permute-start(bf16[128,512]{1,0:T(8,128)(2,1)S(1)} %slice.28), channel_id=1, source_target_pairs={{0,32},{16,48},{32,0},{48,16},{1,33},{17,49},{33,1},{49,17},{2,34}... | collective-permute-start | bytes 393224 | tf_op jit(solution)/shard_map/ppermute | solution.py:211
  53.2 7.6 %collective-permute-start.4 = (bf16[128,512]{1,0:T(8,128)(2,1)S(1)}, bf16[128,512]{1,0:T(8,128)(2,1)S(1)}, u32[]{:S(2)}, u32[]{:S(2)}) collective-permute-start(bf16[128,512]{1,0:T(8,128)(2,1)S(1)} %slice.28), channel_id=1, source_target_pairs={{0,48},{16,0},{32,16},{48,32},{1,49},{17,1},{33,17},{49,33},{2,50}... | collective-permute-start | bytes 393224 | tf_op jit(solution)/shard_map/ppermute | solution.py:211
  61.7 3.9 %collective-permute-start.1 = (bf16[4,144,512]{2,1,0:T(8,128)(2,1)S(1)}, bf16[4,144,512]{2,1,0:T(8,128)(2,1)S(1)}, u32[]{:S(2)}, u32[]{:S(2)}) collective-permute-start(bf16[4,144,512]{2,1,0:T(8,128)(2,1)S(1)} %all-to-all-done.same_ref), channel_id=1, source_target_pairs={{0,1},{1,0},{2,3},{3,2},{4,5},{5,4},{6,7},{7,6},{8,9},{9,8},{10,11... | collective-permute-start | bytes 1769480 | tf_op jit(solution)/shard_map/ppermute | solution.py:217
  94.3 27.1 %all-to-all-start.2 = ((bf16[32,32,128]{2,1,0:T(8,128)(2,1)}), bf16[32,32,128]{2,1,0:T(8,128)(2,1)S(1)}, u32[]{:S(2)}, u32[]{:S(2)}) async-start(bf16[32,32,128]{2,1,0:T(8,128)(2,1)} %broadcast_in_dim.11), calls=%async_computation.2 | async-start | bytes 524288 | tf_op jit(solution)/shard_map/all_to_all | solution.py:236
Sparse Core Ops, SparseCore 0:
  10.2 46.6 all-gather.6
  61.8 41.4 all-gather.4
